TPU v7x, 256 devices: a whole 4x4x8 slice. The times are simulated.
256 devices in a mesh: row: 16 (over z_lo, x), col: 16 (over z_hi, y, core).
Axes of the slice: x: 4, y: 4, z: 8 (z_hi: 2, z_lo: 4; z = z_hi * 4 + z_lo), core: 2. Of those that a mesh axis runs over, the one named last changes fastest.
Arguments:
- inverse_tiles: bfloat16 [16384, 16384], P('row', 'col'), may hold values from -0.046875 to 0.046875
- factor: bfloat16 [16384, 4, 512], P('row', None, 'col'), may hold values from -0.75 to 0.75
- inverse_diag: float32 [4, 512, 512], P(None, 'row', 'col'), may hold values from -6 to 6
- tile_list: int32 [4, 128], replicated, may hold values from 0 to 127, as said below
- tile_count: int32 [4], replicated, may hold values from 86 to 128, as said below
Outputs:
- inverse_panel: bfloat16 [16384, 4, 512], P(('row', 'col'))
- diag_block: float32 [4, 512, 512], P(None, 'row', 'col')
Inputs may be any that keep to these rules, and one draw needn't show every extreme that they name: For each supernode the first tile_count entries of tile_list name distinct tiles in increasing order; the remaining entries name the tiles that are not listed. `tile_count`: some supernode lists all 128 tiles.
All inputs are finite; a program needn't handle non-finite values.
Results may differ from a plain program's by a relative error of at most 0.014.
Values may be sent and summed in bfloat16 or wider, within the bound.
A program may use at most 64 MiB of HBM per device.

v0:
```python
import jax
import jax.numpy as jnp
from jax import lax
from jax.sharding import Mesh
from jax.sharding import PartitionSpec as P

TILE = 128
COL = ("col_0", "col_1", "col_2")
ROW_COL = ("row", "col_0", "col_1", "col_2")


def spread(x, axis, root):
    mine = lax.axis_index(axis) == root
    return lax.psum(jnp.where(mine, x, jnp.zeros_like(x)), axis)


def split_up(x, dim, size):
    before, after = (x.shape[:dim], x.shape[dim + 1 :])
    return jnp.moveaxis(x.reshape(*before, size, -1, *after), dim, 0)


def summed_rows(x, chips, core, dim):
    sizes = (lax.axis_size(chips), lax.axis_size(core))
    blocks = split_up(x, dim, sizes[0] * sizes[1])
    inside = blocks.shape[1:]
    blocks = blocks.reshape(*sizes, *inside).swapaxes(0, 1).reshape(-1, *inside)
    blocks = lax.psum_scatter(blocks, core, scatter_dimension=0, tiled=True)
    return lax.psum_scatter(blocks, chips, scatter_dimension=0, tiled=True)[0]


def sent_and_summed(x, axis, dim):
    blocks = split_up(x, dim, lax.axis_size(axis))
    arrived = lax.all_to_all(blocks, axis, split_axis=0, concat_axis=0, tiled=True)
    return arrived.astype(jnp.float32).sum(axis=0)


def per_device(inverse_tiles, factor, inverse_diag, tile_list, tile_count):
    row_devices = lax.axis_size("row")
    col_devices = lax.axis_size(COL)
    row_index = lax.axis_index("row")
    col_index = lax.axis_index(COL)
    rows_blk = inverse_tiles.shape[0]
    cols_blk = inverse_tiles.shape[1]
    supers = factor.shape[1]
    panel_width = factor.shape[2] * col_devices
    tile_total = tile_list.shape[1]
    position = jnp.arange(tile_total, dtype=jnp.int32)
    matches = (tile_list[:, :, None] == position[None, None, :]) & (
        position[None, :, None] < tile_count[:, None, None]
    )
    listed = jnp.any(matches, axis=1).astype(jnp.float32)
    live_all = jnp.repeat(listed, TILE, axis=1)
    row_live = lax.dynamic_slice_in_dim(live_all, row_index * rows_blk, rows_blk, 1).T
    row_factor = lax.all_gather(factor, COL, axis=2, tiled=True)
    row_factor = jnp.where(row_live[:, :, None] > 0, row_factor, jnp.zeros_like(row_factor))
    blocks_per = row_devices // col_devices
    received = spread(row_factor, "row", col_index * blocks_per + 0)
    col_factor = received.reshape(cols_blk, supers * panel_width)
    whole_term = jnp.dot(inverse_tiles, col_factor, preferred_element_type=jnp.float32).reshape(
        rows_blk, supers, panel_width
    )
    panel_cols = summed_rows(whole_term, ("col_0", "col_1"), "col_2", 2)
    panel_cols = -panel_cols * row_live[:, :, None]
    diag_part = jnp.einsum(
        "rsv,rsw->svw", row_factor.astype(jnp.float32), panel_cols, precision=lax.Precision.HIGHEST
    )
    diag_mine = sent_and_summed(diag_part.astype(jnp.bfloat16), "row", 1)
    inverse_panel = lax.all_to_all(
        panel_cols.astype(jnp.bfloat16), COL, split_axis=0, concat_axis=2, tiled=True
    )
    diag_block = inverse_diag - diag_mine
    return (inverse_panel, diag_block)


def solution(mesh):
    torus = Mesh(
        mesh.devices.reshape(mesh.shape["row"], 2, 4, 2), ("row", "col_0", "col_1", "col_2")
    )
    return jax.shard_map(
        per_device,
        mesh=torus,
        in_specs=(P("row", COL), P("row", None, COL), P(None, "row", COL), P(), P()),
        out_specs=(P(ROW_COL, None, None), P(None, "row", COL)),
        check_vma=False,
    )
```

profile of v0, /device:TPU:32, one launch (start us, length us, event | category | flops | bytes accessed | tf_op | source)
XLA Modules:
  0.0 482.2 jit_solution(6248333700501249892)
XLA Ops:
  7.2 0.7 all-gather.2.cloned.1.call-update
  8.0 0.7 iota_compare_fusion.1
  8.7 0.9 fusion.6
  9.9 79.6 %all-gather.2.cloned.1.call-done = bf16[1024,4,512]{0,2,1:T(8,128)(2,1)} async-done(((bf16[1024,4,32]{0,2,1:T(8,128)(2,1)}), bf16[1024,4,512]{0,2,1:T(8,128)(2,1)}) %all-gather.2.cloned.1.call-update) | async-done | bytes 4194320 | tf_op jit(solution)/shard_map/all_gather | solution.py:54
  89.5 4.5 broadcast_select_fusion.1
  94.1 169.6 %all-reduce.2.cloned.1.call-done = bf16[1024,2048]{0,1:T(8,128)(2,1)} async-done(((bf16[1024,2048]{0,1:T(8,128)(2,1)}), bf16[1024,2048]{0,1:T(8,128)(2,1)}) %all-reduce.2.cloned.1.call-update) | async-done | bytes 4194320 | tf_op jit(solution)/shard_map/psum | solution.py:14
  263.7 6.4 %fusion.9 = f32[2048,1024]{1,0:T(8,128)S(1)} fusion(bf16[1024,2048]{0,1:T(8,128)(2,1)} %all-reduce.2.cloned.1.call-done, bf16[1024,1024]{1,0:T(8,128)(2,1)S(1)} %copy-done), kind=kOutput, calls=%fused_computation.20 | convolution fusion | flops 4294967296 | bytes 14680064 | tf_op jit(solution)/shard_map/dot_general | solution.py:59
  270.1 4.1 copy.38
  274.3 25.8 %reduce-scatter.3.cloned.1.call-done = f32[8,1024,4,32]{1,3,2,0:T(8,128)} async-done(((f32[16,1024,4,32]{1,3,2,0:T(8,128)}), f32[8,1024,4,32]{1,3,2,0:T(8,128)}) %reduce-scatter.3.cloned.1.call-update) | async-done | bytes 4194320 | tf_op jit(solution)/shard_map/reduce_scatter | solution.py:27
  300.1 131.2 %reduce-scatter.5.cloned.1.call-done = f32[1,1024,4,32]{1,3,2,0:T(8,128)} async-done(((f32[8,1024,4,32]{1,3,2,0:T(8,128)}), f32[1,1024,4,32]{1,3,2,0:T(8,128)}) %reduce-scatter.5.cloned.1.call-update) | async-done | bytes 524304 | tf_op jit(solution)/shard_map/reduce_scatter | solution.py:28
  431.3 6.0 %fusion.2 = bf16[4,512,32]{1,2,0:T(8,128)(2,1)S(1)} fusion(bf16[1024,4,512]{0,2,1:T(8,128)(2,1)} %all-gather.2.cloned.1.call-done, pred[1024,4]{0,1:T(4,128)(4,1)S(1)} %get-tuple-element.12, f32[1,1024,4,32]{1,3,2,0:T(8,128)} %reduce-scatter.5.cloned.1.call-done, f32[1024,4]{0,1:T(4,128)S(1)} %get-tuple-element.13), kind=kOutput, calls=%fused_computation.4 | convolution fusion | flops 807731200 | bytes 4870144 | tf_op jit(solution)/shard_map/rsv,rsw->svw/dot_general | solution.py:64
  437.7 1.2 reshape.56
  438.9 5.8 %all-to-all-start.1 = ((bf16[16,2,2048]{2,1,0:T(2,128)(2,1)}), bf16[16,2,2048]{2,1,0:T(2,128)(2,1)S(1)}, u32[]{:S(2)}, u32[]{:S(2)}) async-start(bf16[16,2,2048]{2,1,0:T(2,128)(2,1)} %reshape.56), calls=%async_computation.3 | async-start | bytes 262144 | tf_op jit(solution)/shard_map/all_to_all | solution.py:33
  444.7 1.1 fusion.3
  445.8 0.7 copy.39
  446.5 1.7 reshape.54
  448.2 3.4 all-to-all-done.1
  451.6 5.4 %all-to-all-start = ((bf16[16,2,4096]{2,1,0:T(2,128)(2,1)}), bf16[16,2,4096]{2,1,0:T(2,128)(2,1)S(1)}, u32[]{:S(2)}, u32[]{:S(2)}) async-start(bf16[16,2,4096]{2,1,0:T(2,128)(2,1)} %reshape.54), calls=%async_computation.2 | async-start | bytes 524288 | tf_op jit(solution)/shard_map/all_to_all | solution.py:68
  457.0 0.9 copy.45
  458.3 0.7 copy.47
  459.1 12.7 %all-to-all-done = bf16[16,2,4096]{2,1,0:T(2,128)(2,1)S(1)} async-done(((bf16[16,2,4096]{2,1,0:T(2,128)(2,1)}), bf16[16,2,4096]{2,1,0:T(2,128)(2,1)S(1)}, u32[]{:S(2)}, u32[]{:S(2)}) %all-to-all-start) | async-done | bytes 262176 | tf_op jit(solution)/shard_map/all_to_all | solution.py:68
  471.8 0.5 reshape.55
  472.3 1.3 copy.50
  473.6 2.0 copy.46
  (18 shorter events, 1.4 us)
Async XLA Ops:
  7.2 256.6 %copy-start = (bf16[1024,1024]{1,0:T(8,128)(2,1)S(1)}, bf16[1024,1024]{1,0:T(8,128)(2,1)}, u32[]{:S(2)}) copy-start(bf16[1024,1024]{1,0:T(8,128)(2,1)} %param.5) | copy-start | bytes 6291460
  7.2 82.4 %all-gather.2.cloned.1.call-start = ((), (), s32[]{:S(2)}) async-start(), calls=%async_computation.4 | async-start | bytes 4456448 | tf_op jit(solution)/shard_map/all_gather | solution.py:54
  7.9 255.8 %all-reduce.2.cloned.1.call-start = ((), (), s32[]{:S(2)}) async-start(), calls=%async_computation.5 | async-start | bytes 8388608 | tf_op jit(solution)/shard_map/psum | solution.py:14
  94.1 206.0 %reduce-scatter.3.cloned.1.call-start = ((), (), s32[]{:S(2)}) async-start(), calls=%async_computation.6 | async-start | bytes 12582912 | tf_op jit(solution)/shard_map/reduce_scatter | solution.py:27
  274.2 157.1 %reduce-scatter.5.cloned.1.call-start = ((), (), s32[]{:S(2)}) async-start(), calls=%async_computation.7 | async-start | bytes 4718592 | tf_op jit(solution)/shard_map/reduce_scatter | solution.py:28
  438.9 12.7 %all-to-all-start.1 = ((bf16[16,2,2048]{2,1,0:T(2,128)(2,1)}), bf16[16,2,2048]{2,1,0:T(2,128)(2,1)S(1)}, u32[]{:S(2)}, u32[]{:S(2)}) async-start(bf16[16,2,2048]{2,1,0:T(2,128)(2,1)} %reshape.56), calls=%async_computation.3 | async-start | bytes 262144 | tf_op jit(solution)/shard_map/all_to_all | solution.py:33
  451.6 20.2 %all-to-all-start = ((bf16[16,2,4096]{2,1,0:T(2,128)(2,1)}), bf16[16,2,4096]{2,1,0:T(2,128)(2,1)S(1)}, u32[]{:S(2)}, u32[]{:S(2)}) async-start(bf16[16,2,4096]{2,1,0:T(2,128)(2,1)} %reshape.54), calls=%async_computation.2 | async-start | bytes 524288 | tf_op jit(solution)/shard_map/all_to_all | solution.py:68
Sparse Core Ops, SparseCore 0:
  10.8 78.7 all-gather.1
  94.2 169.4 all-reduce.1
  274.3 25.6 reduce-scatter.2
  304.6 126.5 reduce-scatter.4
where the time goes:
time: 483 us; the launch traced here: 482 us
  waiting for transfers between devices  423 us (88%)
  local copies, waits for them, and re-layouts  14.1 us (3%)
  between operations  13.9 us (3%)
  matrix products  12.3 us (3%)
  starting transfers between devices  11.4 us (2%)
  other arithmetic  7.39 us (2%)
    psum x1, waiting for transfers between devices, spread(): return lax.psum(jnp.where(mine, x, jnp.zeros_like(x)), axis)  170 us
    reduce_scatter x1, waiting for transfers between devices, summed_rows(): return lax.psum_scatter(blocks, chips, scatter_dimension=0, tiled=True)[0]  131 us
    all_gather x1, waiting for transfers between devices, per_device(): row_factor = lax.all_gather(factor, COL, axis=2, tiled=True)  79.6 us
    reduce_scatter x1, waiting for transfers between devices, summed_rows(): blocks = lax.psum_scatter(blocks, core, scatter_dimension=0, tiled=True)  25.8 us
    all_to_all x1, waiting for transfers between devices, per_device(): lax.all_to_all(panel_cols.astype(jnp.bfloat16), COL, split_axis=0, concat...  12.7 us
  transfers between devices with their start and end apart: 6, of which 6 were waited for; matrix products, arithmetic and copies ran while one was open for 2% of the time, Pallas kernels for 0%

commit v1 on v0

v1 whole, which is shorter than its diff:
```python
import jax
import jax.numpy as jnp
from jax import lax
from jax.experimental import pallas as pl
from jax.experimental.pallas import tpu as pltpu
from jax.sharding import PartitionSpec as P

MESH = pl.DeviceIdType.MESH
F32 = jnp.float32
BF16 = jnp.bfloat16
NT_DIMS = (((1,), (1,)), ((), ()))


def div(a, b):
    return lax.div(a, jnp.int32(b))


def rem(a, b):
    return lax.rem(a, jnp.int32(b))


def kernel(
    list_ref, count_ref, a_ref, ft_ref, inv_ref, panel_ref, diag_ref,
    abuf, fmask, fg, fr, pp, pyr, zown, zs, zr, pb, cr, ds, dyr, dxs, dxr, dzs, dzr, perm,
    sems,
):
    row, col = lax.axis_index("row"), lax.axis_index("col")
    zl, x = div(row, 4), rem(row, 4)
    zh, y, k = div(col, 8), rem(div(col, 2), 4), rem(col, 2)
    z, t = zh * 4 + zl, zh * 4 + y

    def at(zl_=zl, x_=x, zh_=zh, y_=y, k_=k):
        return (zl_ * 4 + x_, zh_ * 8 + y_ * 2 + k_)

    used = [0]

    def take(n=1):
        used[0] += n
        return used[0] - n

    def remote(src, dst, send, recv, device):
        return pltpu.make_async_remote_copy(
            src_ref=src, dst_ref=dst, send_sem=sems.at[send], recv_sem=sems.at[recv],
            device_id=device, device_id_type=MESH,
        )

    partner = at(k_=1 - k)
    around_x = [at(x_=rem(x + o, 4)) for o in (1, 2, 3)]
    around_y = [at(y_=rem(y + o, 4)) for o in (1, 2, 3)]
    right, left = around_x[0], around_x[2]

    def chip_t(t_):
        return at(zh_=div(t_, 4), y_=rem(t_, 4))

    def chip_z(z_):
        return at(zh_=div(z_, 4), zl_=rem(z_, 4))

    to_zh, to_y, half = div(zl, 2), rem(zl, 2) * 2 + div(x, 2), rem(x, 2)
    group, place = zh * 2 + div(y, 2), rem(y, 2)
    here = (to_zh == zh) & (to_y == y) & (group == x)

    def source(h, p):
        return at(
            zl_=zh * 2 + div(y, 2), x_=rem(y, 2) * 2 + h, zh_=div(x, 2), y_=rem(x, 2) * 2 + p
        )

    barrier = pltpu.get_barrier_semaphore()

    def greet(device):
        pl.semaphore_signal(barrier, inc=1, device_id=device, device_id_type=MESH)

    greet(partner)
    for device in around_x:
        greet(device)
    for o in range(1, 8):
        greet(chip_t(rem(t + o, 8)))
    for o in range(1, 8):
        if o != 4:
            greet(chip_z(rem(z + o, 8)))
    for h in range(2):
        for p in range(2):
            s_row, s_col = source(h, p)
            same = (s_row == row) & (s_col == col)

            @pl.when(jnp.logical_not(same))
            def _():
                greet((s_row, s_col))

    s_iota = lax.broadcasted_iota(jnp.int32, (4, 128), 0)
    p_iota = lax.broadcasted_iota(jnp.int32, (4, 128), 1)
    counts = jnp.zeros((4, 128), jnp.int32)
    for s in range(4):
        counts = jnp.where(s_iota == s, count_ref[s], counts)
    listed = jnp.where(p_iota < counts, list_ref[...], -1)

    def live(tile):
        return jnp.max(jnp.where(listed == tile, 1.0, 0.0), axis=1, keepdims=True)

    for i in range(8):
        alive = live(row * 8 + i)
        for s in range(4):
            block = ft_ref[s, :, i * 128 : (i + 1) * 128]
            keep = jnp.broadcast_to(alive[s : s + 1, :], block.shape) > 0
            fmask[s, :, i * 128 : (i + 1) * 128] = jnp.where(
                keep, block.astype(F32), 0.0
            ).astype(BF16)
    alive = live(row * 8 + t)
    lane_s = rem(div(lax.broadcasted_iota(jnp.int32, (1, 256), 1), 32), 4)
    lane_live = jnp.zeros((1, 256), F32)
    for s in range(4):
        lane_live = jnp.where(lane_s == s, alive[s : s + 1, :], lane_live)

    pl.semaphore_wait(barrier, 21 - jnp.where(here, 1, 0))

    pending = []

    first_recv = take(4)
    direct = []
    for i in range(4):
        target = at(zl_=rem(zl + i, 4), x_=group, zh_=to_zh, y_=to_y)
        direct.append(
            remote(
                fmask, fg.at[group, half, place], take(), first_recv + half * 2 + place, target
            )
        )
    own_copy = pltpu.make_async_copy(
        fmask, fg.at[group, half, place], sems.at[first_recv + half * 2 + place]
    )

    @pl.when(here)
    def _():
        own_copy.start()

    @pl.when(jnp.logical_not(here))
    def _():
        direct[0].start()

    for copy in direct[1:]:
        copy.start()
    pending += direct[1:]

    a_sems = take(3)
    a_mine = pltpu.make_async_copy(a_ref, abuf.at[k], sems.at[a_sems])
    a_mine.start()
    a_swap = remote(a_ref, abuf.at[k], a_sems + 1, a_sems + 2, partner)
    a_swap.start()
    a_theirs = remote(a_ref, abuf.at[1 - k], a_sems + 1, a_sems + 2, partner)

    def rows_of(t_):
        return fmask.at[:, :, pl.ds(pl.multiple_of(t_ * 128, 128), 128)]

    fr_own_sem = take()
    fr_mine = pltpu.make_async_copy(rows_of(t), fr.at[:, t, k], sems.at[fr_own_sem])
    fr_mine.start()
    fr_arrive = []
    for o in range(1, 8):
        t_to, t_from = rem(t + o, 8), rem(t + 8 - o, 8)
        send, recv = take(), take()
        copy = remote(rows_of(t_to), fr.at[:, t, k], send, recv, chip_t(t_to))
        copy.start()
        pending.append(copy)
        fr_arrive.append(remote(rows_of(t), fr.at[:, t_from, k], send, recv, chip_t(t_from)))

    r_iota = lax.broadcasted_iota(jnp.int32, (256, 512), 0)
    c_iota = lax.broadcasted_iota(jnp.int32, (256, 512), 1)
    same_w = rem(r_iota, 32) == rem(c_iota, 32)
    same_s = rem(div(r_iota, 32), 4) == div(c_iota, 128)
    j4 = rem(div(c_iota, 32), 4)
    for core in range(2):
        hit = same_w & same_s & (j4 == div(r_iota, 128) * 2 + core)
        perm[core] = jnp.where(hit, 1.0, 0.0).astype(BF16)

    g_left, g_right, g_far = rem(x + 3, 4), rem(x + 1, 4), rem(x + 2, 4)
    right_send, right_recv = take(4), take(4)
    left_send, left_recv = take(4), take(4)
    far_right_send, far_right_recv = take(2), take(2)
    far_left_send, far_left_recv = take(2), take(2)
    for p in range(2):
        for h in range(2):
            b = h * 2 + p
            s_dev = source(h, p)
            remote(fmask, fg.at[x, h, p], first_recv, first_recv + b, s_dev).wait_recv()
            block = fg.at[x, h, p]
            for send, recv, device in ((right_send, right_recv, right), (left_send, left_recv, left)):
                copy = remote(block, block, send + b, recv + b, device)
                copy.start()
                pending.append(copy)

    def partial(step, g):
        def body(i, carry):
            rows = pl.ds(pl.multiple_of(i * 256, 256), 256)
            acc = lax.dot_general(
                abuf[0, rows], fg[g, 0].reshape(256, 1024), NT_DIMS, preferred_element_type=F32
            )
            acc += lax.dot_general(
                abuf[1, rows], fg[g, 1].reshape(256, 1024), NT_DIMS, preferred_element_type=F32
            )
            first = rem(i, 2) * 2
            for j in range(2):
                pp[step, div(i, 2), first + j] = acc[j * 128 : (j + 1) * 128].astype(BF16)
            return carry

        lax.fori_loop(0, 4, body, 0)

    y_sems = take(24)
    z_sems, c_sems = take(8), take(8)
    dy_send, dy_recv = take(8), take(8)

    def send_y(step):
        for o in (1, 2, 3):
            sem = y_sems + (step * 3 + o - 1) * 2
            copy = remote(
                pp.at[step, :, rem(y + o, 4)], pyr.at[step, o - 1], sem, sem + 1, around_y[o - 1]
            )
            copy.start()
            pending.append(copy)

    def reduce_y(step):
        for o in (1, 2, 3):
            sem = y_sems + (step * 3 + o - 1) * 2
            came = around_y[3 - o]
            remote(pp.at[step, :, y], pyr.at[step, o - 1], sem, sem + 1, came).wait_recv()

        def total(which):
            acc = pp[step, which, y].astype(F32)
            for o in range(3):
                acc += pyr[step, o, which].astype(F32)
            return acc

        zs[step] = total(1 - zh).astype(BF16)
        copy = remote(
            zs.at[step], zr.at[step], z_sems + step * 2, z_sems + step * 2 + 1, at(zh_=1 - zh)
        )
        copy.start()
        pending.append(copy)
        zown[step] = total(zh)
        return copy

    def finish(step, g, z_copy):
        z_copy.wait_recv()
        panel = -(zown[step] + zr[step].astype(F32))
        panel = jnp.where(lane_live > 0, panel, 0.0)
        pb[step] = panel.astype(BF16)
        theirs = pb.at[step, pl.ds(pl.multiple_of((1 - k) * 64, 64), 64)]
        copy = remote(theirs, cr.at[step], c_sems + step * 2, c_sems + step * 2 + 1, partner)
        copy.start()
        pending.append(copy)
        acc = jnp.zeros((512, 256), F32)
        for s in range(4):
            part = jnp.where(lane_s == s, panel, 0.0).astype(BF16)
            acc += jnp.dot(fr[s].reshape(512, 128), part, preferred_element_type=F32)
        for p in range(2):
            ds[step, p] = acc[:, p * 128 : (p + 1) * 128].astype(BF16)
            y_to, zh_to = rem(g, 2) * 2 + p, div(g, 2)

            @pl.when(y_to == y)
            def _():
                dyr[zh_to, y] = ds[step, p]

            send = remote(
                ds.at[step, p], dyr.at[zh_to, y], dy_send + step * 2 + p,
                dy_recv + zh_to * 4 + y, at(y_=y_to),
            )

            @pl.when(y_to != y)
            def _():
                send.start()

            pending.append((y_to != y, send))
        return copy

    def write_panel(step, g, c_copy):
        c_copy.wait_recv()
        mine = pb[step, pl.ds(pl.multiple_of(k * 64, 64), 64)]
        res = jnp.dot(mine, perm[k], preferred_element_type=F32)
        res += jnp.dot(cr[step], perm[1 - k], preferred_element_type=F32)
        for s in range(4):
            lanes = pl.ds(pl.multiple_of(s * 512 + g * 128, 128), 128)
            panel_ref[:, lanes] = res[:, s * 128 : (s + 1) * 128].astype(BF16)

    a_mine.wait()
    a_theirs.wait_recv()
    pending.append(a_swap)
    partial(0, x)
    send_y(0)

    def came_from_left(h, p):
        b = h * 2 + p
        block = fg.at[g_left, h, p]
        remote(block, block, right_send + b, right_recv + b, left).wait_recv()
        if p == 0:
            copy = remote(block, block, far_right_send + h, far_right_recv + h, right)
            copy.start()
            pending.append(copy)

    def came_from_right(h, p):
        b = h * 2 + p
        block = fg.at[g_right, h, p]
        remote(block, block, left_send + b, left_recv + b, right).wait_recv()
        if p == 1:
            copy = remote(block, block, far_left_send + h, far_left_recv + h, left)
            copy.start()
            pending.append(copy)

    for h in range(2):
        came_from_left(h, 0)
    for h in range(2):
        came_from_right(h, 0)
    for h in range(2):
        came_from_left(h, 1)
        came_from_right(h, 1)
    partial(1, g_left)
    send_y(1)
    partial(2, g_right)
    send_y(2)

    fr_mine.wait()
    for copy in fr_arrive:
        copy.wait_recv()
    fr_sems = take(2)
    fr_swap = remote(fr.at[:, :, k], fr.at[:, :, k], fr_sems, fr_sems + 1, partner)
    fr_swap.start()
    pending.append(fr_swap)
    z0 = reduce_y(0)
    z1 = reduce_y(1)
    z2 = reduce_y(2)
    remote(fr.at[:, :, 1 - k], fr.at[:, :, 1 - k], fr_sems, fr_sems + 1, partner).wait_recv()
    c0 = finish(0, x, z0)
    c1 = finish(1, g_left, z1)
    c2 = finish(2, g_right, z2)

    for h in range(2):
        block = fg.at[g_far, h, 0]
        remote(block, block, far_right_send + h, far_right_recv + h, left).wait_recv()
        block = fg.at[g_far, h, 1]
        remote(block, block, far_left_send + h, far_left_recv + h, right).wait_recv()
    partial(3, g_far)
    send_y(3)
    write_panel(0, x, c0)
    write_panel(1, g_left, c1)
    write_panel(2, g_right, c2)
    z3 = reduce_y(3)
    c3 = finish(3, g_far, z3)
    write_panel(3, g_far, c3)

    for zh_ in range(2):
        for o in (1, 2, 3):
            y_from = rem(y + o, 4)
            remote(
                ds.at[0, 0], dyr.at[zh_, y_from], dy_send, dy_recv + zh_ * 4 + y_from,
                around_y[o - 1],
            ).wait_recv()
    for zh_ in range(2):
        for zl_ in range(4):
            rows = slice(zl_ * 128, (zl_ + 1) * 128)
            acc = dyr[zh_, 0, rows].astype(F32)
            for y_ in range(1, 4):
                acc += dyr[zh_, y_, rows].astype(F32)
            for x_ in range(4):
                dxs[x_, zh_, zl_] = acc[x_ * 32 : (x_ + 1) * 32].astype(BF16)
    arrive = []
    for o in (1, 2, 3):
        send, recv = take(), take()
        copy = remote(dxs.at[rem(x + o, 4)], dxr.at[o - 1], send, recv, around_x[o - 1])
        copy.start()
        pending.append(copy)
        arrive.append(remote(dxs.at[x], dxr.at[o - 1], send, recv, around_x[3 - o]))
    for copy in arrive:
        copy.wait_recv()
    acc = dxs[x].astype(F32)
    for o in range(3):
        acc += dxr[o].astype(F32)
    dzs[...] = acc.astype(BF16)
    arrive = []
    for o in range(1, 8):
        z_to, z_from = rem(z + o, 8), rem(z + 8 - o, 8)
        send, recv = take(), take()
        copy = remote(
            dzs.at[div(z_to, 4), rem(z_to, 4)], dzr.at[o - 1], send, recv, chip_z(z_to)
        )
        copy.start()
        pending.append(copy)
        arrive.append(remote(dzs.at[zh, zl], dzr.at[o - 1], send, recv, chip_z(z_from)))
    for copy in arrive:
        copy.wait_recv()
    total = dzs[zh, zl].astype(F32)
    for o in range(7):
        total += dzr[o].astype(F32)
    for s in range(4):
        diag_ref[s] = inv_ref[s] - total[:, s * 32 : (s + 1) * 32]

    @pl.when(jnp.logical_not(here))
    def _():
        direct[0].wait_send()

    for copy in pending:
        if isinstance(copy, tuple):
            sent, copy = copy
            pl.when(sent)(copy.wait_send)
        else:
            copy.wait_send()
    assert used[0] <= SEMS, used


SEMS = 136


def per_device(inverse_tiles, factor, inverse_diag, tile_list, tile_count):
    vmem = pl.BlockSpec(memory_space=pltpu.VMEM)
    v = pltpu.VMEM
    panel, diag = pl.pallas_call(
        kernel,
        out_shape=(
            jax.ShapeDtypeStruct((64, 2048), BF16),
            jax.ShapeDtypeStruct((4, 32, 32), F32),
        ),
        in_specs=[
            vmem,
            pl.BlockSpec(memory_space=pltpu.SMEM),
            pl.BlockSpec(memory_space=pl.ANY),
            vmem,
            vmem,
        ],
        out_specs=(vmem, vmem),
        scratch_shapes=[
            v((2, 1024, 1024), BF16),
            v((4, 32, 1024), BF16),
            v((4, 2, 2, 4, 32, 1024), BF16),
            v((4, 8, 2, 32, 128), BF16),
            v((4, 2, 4, 128, 256), BF16),
            v((4, 3, 2, 128, 256), BF16),
            v((4, 128, 256), F32),
            v((4, 128, 256), BF16),
            v((4, 128, 256), BF16),
            v((4, 128, 256), BF16),
            v((4, 64, 256), BF16),
            v((4, 2, 512, 128), BF16),
            v((2, 4, 512, 128), BF16),
            v((4, 2, 4, 32, 128), BF16),
            v((3, 2, 4, 32, 128), BF16),
            v((2, 4, 32, 128), BF16),
            v((7, 32, 128), BF16),
            v((2, 256, 512), BF16),
            pltpu.SemaphoreType.DMA((SEMS,)),
        ],
        compiler_params=pltpu.CompilerParams(
            collective_id=0, has_side_effects=True, vmem_limit_bytes=48 * 1024 * 1024
        ),
        cost_estimate=pl.CostEstimate(
            flops=2 * 1024 * 2048 * 1024, bytes_accessed=4 << 20, transcendentals=0
        ),
    )(tile_list, tile_count, inverse_tiles, jnp.transpose(factor, (1, 2, 0)), inverse_diag)
    return panel.reshape(64, 4, 512), diag


def solution(mesh):
    return jax.shard_map(
        per_device,
        mesh=mesh,
        in_specs=(P("row", "col"), P("row", None, "col"), P(None, "row", "col"), P(), P()),
        out_specs=(P(("row", "col"), None, None), P(None, "row", "col")),
        check_vma=False,
    )
```

time: 483 us -> 154 us (0.32)
  waiting for transfers between devices: 423 us -> 0 us
  Pallas kernels: 0 us -> 144 us
  between operations: 13.9 us -> 0.65 us
  matrix products: 12.3 us -> 0 us
  starting transfers between devices: 11.4 us -> 0 us
  local copies, waits for them, and re-layouts: 14.1 us -> 6.22 us
  other arithmetic: 7.39 us -> 0 us
    psum x1 -> x0, waiting for transfers between devices: 170 us -> none  [spread(): return lax.psum(jnp.where(mine, x, jnp.zeros_like(x)), axis)]
    reduce_scatter x2 -> x0, waiting for transfers between devices: 157 us -> none  [the longest x1 131 us: summed_rows(): return lax.psum_scatter(blocks, chips, scatter_dimension=0, tiled=True)[0]]
    pallas_call x0 -> x1, Pallas kernels: none -> 144 us  [per_device(): pl.pallas_call(kernel, out_shape=(jax.ShapeDtypeStruct((64, 2048), BF16),...]
    all_gather x1 -> x0, waiting for transfers between devices: 79.6 us -> none  [per_device(): row_factor = lax.all_gather(factor, COL, axis=2, tiled=True)]
    all_to_all x2 -> x0, waiting for transfers between devices: 16.1 us -> none  [the longest x1 12.7 us: per_device(): lax.all_to_all(panel_cols.astype(jnp.bfloat16), COL, split_axis=0, concat...]
    dot_general x2 -> x0, matrix products: 12.3 us -> none  [the longest x1 6.36 us: per_device(): jnp.dot(inverse_tiles, col_factor, preferred_element_type=jnp.float32)]
    all_to_all x2 -> x0, starting transfers between devices: 11.2 us -> none  [the longest x1 5.77 us: sent_and_summed(): lax.all_to_all(blocks, axis, split_axis=0, concat_axis=0, tiled=True)]
  transfers between devices with their start and end apart: 6 -> 0, of which waited for: 6 -> 0; matrix products, arithmetic and copies ran while one was open for 2% -> 0% of each run, Pallas kernels for 0% -> 0%
where the time goes in v1:
time: 154 us; the launch traced here: 151 us
  Pallas kernels  144 us (94%)
  local copies, waits for them, and re-layouts  6.22 us (4%)
    pallas_call x1, Pallas kernels, per_device(): pl.pallas_call(kernel, out_shape=(jax.ShapeDtypeStruct((64, 2048), BF16),...  144 us
    unnamed x11, local copies, waits for them, and re-layouts  5.34 us

profile of v1, /device:TPU:32, one launch (start us, length us, event | category | flops | bytes accessed | tf_op | source)
XLA Modules:
  0.0 151.4 jit_solution(15583438189533474419)
XLA Ops:
  0.6 0.0 copy-start
  0.6 1.6 %copy-done = bf16[1024,1024]{1,0:T(8,128)(2,1)S(1)} copy-done((bf16[1024,1024]{1,0:T(8,128)(2,1)S(1)}, bf16[1024,1024]{1,0:T(8,128)(2,1)}, u32[]{:S(2)}) %copy-start) | copy-done | bytes 2097176
  2.2 0.0 copy-start.1
  2.2 0.9 copy-done.1
  3.2 0.0 copy-start.2
  3.2 0.8 copy-done.2
  4.0 0.0 copy-start.3
  4.0 0.7 copy-done.3
  4.7 0.0 copy-start.4
  4.7 0.7 copy-done.4
  5.4 144.5 %shard_map.68 = (bf16[64,2048]{1,0:T(8,128)(2,1)S(1)}, f32[4,32,32]{2,1,0:T(8,128)S(1)}) custom-call(s32[4,128]{1,0:T(4,128)S(1)} %copy-done.3, s32[4]{0:T(128)S(1)} %copy-done.4, bf16[1024,1024]{1,0:T(8,128)(2,1)S(1)} %copy-done, bf16[4,32,1024]{2,1,0:T(8,128)(2,1)S(1)} %bitcast.1, f32[4,32,32]{2,1,0:T(8,128)S(1)} %copy-done.2), custom_call_target="tpu_custom_call" | custom-call | flops 4294967296 | bytes 4194304 | tf_op jit(solution)/shard_map/pallas_call | solution.py:411
  149.9 0.9 reshape.7
  150.7 0.6 copy.8
Async XLA Ops:
  0.6 1.6 %copy-start = (bf16[1024,1024]{1,0:T(8,128)(2,1)S(1)}, bf16[1024,1024]{1,0:T(8,128)(2,1)}, u32[]{:S(2)}) copy-start(bf16[1024,1024]{1,0:T(8,128)(2,1)} %a_ref.1) | copy-start | bytes 6291460
  2.2 0.9 copy-start.1
  3.2 0.8 copy-start.2
  4.0 0.7 copy-start.3
  4.7 0.7 copy-start.4

commit v2 on v1

v2 whole, which is shorter than its diff:
```python
import jax
import jax.numpy as jnp
from jax import lax
from jax.experimental import pallas as pl
from jax.experimental.pallas import tpu as pltpu
from jax.sharding import PartitionSpec as P

MESH = pl.DeviceIdType.MESH
F32 = jnp.float32
BF16 = jnp.bfloat16
NT_DIMS = (((1,), (1,)), ((), ()))


def div(a, b):
    return lax.div(a, jnp.int32(b))


def rem(a, b):
    return lax.rem(a, jnp.int32(b))


def kernel(
    list_hbm, count_hbm, a_ref, ft_hbm, inv_hbm, panel_ref, diag_ref,
    list_ref, count_ref, ft_ref, inv_ref,
    abuf, fmask, ftile, zbuf, fg, fr, pp, pyr, zown, zs, zr, pb, cr, ds, dyr, dxs, dxr, dzs, dzr,
    perm, spread, sems,
):
    row, col = lax.axis_index("row"), lax.axis_index("col")
    zl, x = div(row, 4), rem(row, 4)
    zh, y, k = div(col, 8), rem(div(col, 2), 4), rem(col, 2)
    z, t = zh * 4 + zl, zh * 4 + y

    def at(zl_=zl, x_=x, zh_=zh, y_=y, k_=k):
        return (zl_ * 4 + x_, zh_ * 8 + y_ * 2 + k_)

    used = [0]

    def take(n=1):
        used[0] += n
        return used[0] - n

    def remote(src, dst, send, recv, device):
        return pltpu.make_async_remote_copy(
            src_ref=src, dst_ref=dst, send_sem=sems.at[send], recv_sem=sems.at[recv],
            device_id=device, device_id_type=MESH,
        )

    partner = at(k_=1 - k)
    around_x = [at(x_=rem(x + o, 4)) for o in (1, 2, 3)]
    around_y = [at(y_=rem(y + o, 4)) for o in (1, 2, 3)]
    right, left = around_x[0], around_x[2]

    def chip_t(t_):
        return at(zh_=div(t_, 4), y_=rem(t_, 4))

    def chip_z(z_, x_=x):
        return at(zh_=div(z_, 4), zl_=rem(z_, 4), x_=x_)

    swap_z = jnp.where((z >= 2) & (z <= 5), 7 - z, z)
    moves = swap_z != z
    across = chip_z(swap_z, rem(x + 2, 4))
    u_own, h_own = div(x, 2), rem(x, 2)

    first = take(5)
    loads = [
        pltpu.make_async_copy(src, dst, sems.at[first + i])
        for i, (src, dst) in enumerate(
            ((ft_hbm, ft_ref), (list_hbm, list_ref), (count_hbm, count_ref), (inv_hbm, inv_ref),
             (a_ref, abuf.at[k]))
        )
    ]
    for copy in loads:
        copy.start()

    barrier = pltpu.get_barrier_semaphore()

    def greet(device):
        pl.semaphore_signal(barrier, inc=1, device_id=device, device_id_type=MESH)

    greet(partner)
    for device in around_x:
        greet(device)
    for o in range(1, 8):
        greet(chip_t(rem(t + o, 8)))
    for o in range(1, 8):
        if o != 4:
            greet(chip_z(rem(z + o, 8)))

    @pl.when(moves)
    def _():
        greet(across)

    for copy in loads[:3]:
        copy.wait()

    s_iota = lax.broadcasted_iota(jnp.int32, (4, 128), 0)
    p_iota = lax.broadcasted_iota(jnp.int32, (4, 128), 1)
    counts = jnp.zeros((4, 128), jnp.int32)
    for s in range(4):
        counts = jnp.where(s_iota == s, count_ref[s], counts)
    listed = jnp.where(p_iota < counts, list_ref[...], -1)

    def live(tile):
        return jnp.max(jnp.where(listed == tile, 1.0, 0.0), axis=1, keepdims=True)

    for i in range(8):
        alive = live(row * 8 + i)
        for s in range(4):
            block = ft_ref[s, :, i * 128 : (i + 1) * 128]
            keep = jnp.broadcast_to(alive[s : s + 1, :], block.shape) > 0
            block = jnp.where(keep, block.astype(F32), 0.0).astype(BF16)
            fmask[s, :, i * 128 : (i + 1) * 128] = block
            ftile[i, s] = block
    alive = live(row * 8 + t)

    pl.semaphore_wait(barrier, 17 + jnp.where(moves, 1, 0))

    pending = []

    hop_send, hop_recv = take(2), take(2)
    kept = fmask.at[pl.ds(u_own * 2, 2)]
    given = fmask.at[pl.ds((1 - u_own) * 2, 2)]
    zl_there = rem(swap_z, 4)
    local_kept = pltpu.make_async_copy(kept, zbuf.at[zl, u_own], sems.at[hop_recv])
    remote_kept = remote(kept, zbuf.at[zl_there, u_own], hop_send, hop_recv, chip_z(swap_z))

    @pl.when(moves)
    def _():
        remote_kept.start()

    @pl.when(jnp.logical_not(moves))
    def _():
        local_kept.start()

    pending.append((moves, remote_kept))
    gift = remote(given, zbuf.at[zl_there, u_own], hop_send + 1, hop_recv + 1, across)
    gift.start()
    pending.append(gift)

    a_sems = take(2)
    a_swap = remote(a_ref, abuf.at[k], a_sems, a_sems + 1, partner)
    a_swap.start()
    pending.append(a_swap)
    a_theirs = remote(a_ref, abuf.at[1 - k], a_sems, a_sems + 1, partner)

    line_send, line_recv = take(6), take(6)

    def held(i):
        if i == 0:
            return zl
        if i == 1:
            return zl + 1 - 2 * rem(zl, 2)
        if i == 2:
            return rem(zl + 2, 4)
        return 3 - zl

    remote(kept, zbuf.at[zl, u_own], hop_send, hop_recv, chip_z(swap_z)).wait_recv()
    remote(given, zbuf.at[zl, 1 - u_own], hop_send + 1, hop_recv + 1, across).wait_recv()
    for i in (1, 2, 3):
        for b in range(2):
            sem = (i - 1) * 2 + b
            copy = remote(
                zbuf.at[zl, b], zbuf.at[zl, b], line_send + sem, line_recv + sem,
                at(zl_=held(i)),
            )
            copy.start()
            pending.append(copy)

    r_iota = lax.broadcasted_iota(jnp.int32, (256, 512), 0)
    c_iota = lax.broadcasted_iota(jnp.int32, (256, 512), 1)
    r_y, r_s, r_w = div(r_iota, 64), rem(div(r_iota, 32), 2), rem(r_iota, 32)
    same_w = r_w == rem(c_iota, 32)
    for core in range(2):
        hit = same_w & (r_s == div(c_iota, 256)) & (div(rem(c_iota, 256), 32) == r_y * 2 + core)
        perm[core] = jnp.where(hit, 1.0, 0.0).astype(BF16)
    for half in range(2):
        hit = same_w & (r_y == div(c_iota, 128)) & (div(rem(c_iota, 128), 32) == half * 2 + r_s)
        spread[half] = jnp.where(hit, 1.0, 0.0).astype(BF16)

    y_send, y_recv = take(8), take(8)
    right_send, right_recv, left_send, left_recv = take(8), take(8), take(8), take(8)
    zh_at = [div(zl, 2), 1 - div(zl, 2)]
    for q in range(2):
        for i in (2 * q, 2 * q + 1):
            place = held(i)
            z_from = zh * 4 + place
            z_from = jnp.where((z_from >= 2) & (z_from <= 5), 7 - z_from, z_from)
            for b in range(2):
                block = zbuf.at[place, b]
                if i > 0:
                    sem = (i - 1) * 2 + b
                    remote(
                        block, block, line_send + sem, line_recv + sem, at(zl_=place)
                    ).wait_recv()
                y_to = rem(z_from, 2) * 2 + b
                there = fg.at[x, zh_at[q], y]
                sem = y_recv + q * 4 + y
                stay = pltpu.make_async_copy(block, there, sems.at[sem])
                send = remote(block, there, y_send + i * 2 + b, sem, at(y_=y_to))

                @pl.when(y_to == y)
                def _():
                    stay.start()

                @pl.when(y_to != y)
                def _():
                    send.start()

                pending.append((y_to != y, send))
        for o in (0, 1, 3, 2):
            y_from = rem(y + o, 4)
            block = fg.at[x, zh_at[q], y_from]
            sem = q * 4 + y_from
            remote(block, block, y_send, y_recv + sem, around_y[o - 1]).wait_recv()
            for send, recv, device in (
                (right_send, right_recv, right), (left_send, left_recv, left)
            ):
                copy = remote(block, block, send + sem, recv + sem, device)
                copy.start()
                pending.append(copy)

    fr_own_sem = take()
    fr_mine = pltpu.make_async_copy(ftile.at[t], fr.at[:, t, k], sems.at[fr_own_sem])
    fr_mine.start()
    fr_arrive = []
    for o in range(1, 8):
        t_to, t_from = rem(t + o, 8), rem(t + 8 - o, 8)
        send, recv = take(), take()
        copy = remote(ftile.at[t_to], fr.at[:, t, k], send, recv, chip_t(t_to))
        copy.start()
        pending.append(copy)
        fr_arrive.append(remote(ftile.at[t], fr.at[:, t_from, k], send, recv, chip_t(t_from)))

    g_left, g_right, g_far = rem(x + 3, 4), rem(x + 1, 4), rem(x + 2, 4)
    far_right_send, far_right_recv = take(4), take(4)
    far_left_send, far_left_recv = take(4), take(4)

    def from_left(q, y_):
        block = fg.at[g_left, zh_at[q], y_]
        sem = q * 4 + y_
        remote(block, block, right_send + sem, right_recv + sem, left).wait_recv()
        if y_ < 2:
            sem = q * 2 + y_
            copy = remote(block, block, far_right_send + sem, far_right_recv + sem, right)
            copy.start()
            pending.append(copy)

    def from_right(q, y_):
        block = fg.at[g_right, zh_at[q], y_]
        sem = q * 4 + y_
        remote(block, block, left_send + sem, left_recv + sem, right).wait_recv()
        if y_ >= 2:
            sem = q * 2 + y_ - 2
            copy = remote(block, block, far_left_send + sem, far_left_recv + sem, left)
            copy.start()
            pending.append(copy)

    def neighbours(q):
        for y_ in range(2):
            from_left(q, y_)
            from_right(q, y_ + 2)
        for y_ in range(2):
            from_left(q, y_ + 2)
            from_right(q, y_)

    def far(q):
        for y_ in range(2):
            sem = q * 2 + y_
            block = fg.at[g_far, zh_at[q], y_]
            remote(block, block, far_right_send + sem, far_right_recv + sem, left).wait_recv()
            block = fg.at[g_far, zh_at[q], y_ + 2]
            remote(block, block, far_left_send + sem, far_left_recv + sem, right).wait_recv()

    u_of = [u_own, u_own, 1 - u_own, 1 - u_own]

    def partial(step):
        u, half = u_of[step], zh_at[step % 2]

        def body(i, carry):
            rows = pl.ds(pl.multiple_of(i * 256, 256), 256)
            acc = lax.dot_general(
                abuf[0, rows], fg[2 * u, half].reshape(256, 1024), NT_DIMS,
                preferred_element_type=F32,
            )
            acc += lax.dot_general(
                abuf[1, rows], fg[2 * u + 1, half].reshape(256, 1024), NT_DIMS,
                preferred_element_type=F32,
            )
            first = rem(i, 2) * 2
            for j in range(2):
                pp[step, div(i, 2), first + j] = acc[j * 128 : (j + 1) * 128].astype(BF16)
            return carry

        lax.fori_loop(0, 4, body, 0)

    y_sems = take(24)
    z_sems, c_sems = take(8), take(8)
    dy_send, dy_recv = take(6), take(8)

    def send_y(step):
        for o in (1, 2, 3):
            sem = y_sems + (step * 3 + o - 1) * 2
            copy = remote(
                pp.at[step, :, rem(y + o, 4)], pyr.at[step, o - 1], sem, sem + 1, around_y[o - 1]
            )
            copy.start()
            pending.append(copy)

    def reduce_y(step):
        for o in (1, 2, 3):
            sem = y_sems + (step * 3 + o - 1) * 2
            came = around_y[3 - o]
            remote(pp.at[step, :, y], pyr.at[step, o - 1], sem, sem + 1, came).wait_recv()

        def total(which):
            acc = pp[step, which, y].astype(F32)
            for o in range(3):
                acc += pyr[step, o, which].astype(F32)
            return acc

        zs[step] = total(1 - zh).astype(BF16)
        copy = remote(
            zs.at[step], zr.at[step], z_sems + step * 2, z_sems + step * 2 + 1, at(zh_=1 - zh)
        )
        copy.start()
        pending.append(copy)
        zown[step] = total(zh)
        return copy

    lane_s = rem(div(lax.broadcasted_iota(jnp.int32, (1, 256), 1), 32), 2)
    wide_s = rem(div(lax.broadcasted_iota(jnp.int32, (1, 512), 1), 32), 2)

    def finish(step, z_copy):
        z_copy.wait_recv()
        s_here = lane_s + 2 * u_of[step]
        lane_live = jnp.zeros((1, 256), F32)
        for s in range(4):
            lane_live = jnp.where(s_here == s, alive[s : s + 1, :], lane_live)
        panel = -(zown[step] + zr[step].astype(F32))
        panel = jnp.where(lane_live > 0, panel, 0.0)
        pb[step] = panel.astype(BF16)
        theirs = pb.at[step, pl.ds(pl.multiple_of((1 - k) * 64, 64), 64)]
        copy = remote(theirs, cr.at[step], c_sems + step * 2, c_sems + step * 2 + 1, partner)
        copy.start()
        pending.append(copy)
        return copy

    def products(pair):
        step, u = pair * 2, u_of[pair * 2]
        panel = jnp.dot(pb[step], spread[zh_at[0]], preferred_element_type=F32)
        panel += jnp.dot(pb[step + 1], spread[zh_at[1]], preferred_element_type=F32)
        acc = jnp.zeros((512, 512), F32)
        for s in range(2):
            part = jnp.where(wide_s == s, panel, 0.0).astype(BF16)
            acc += jnp.dot(fr[2 * u + s].reshape(512, 128), part, preferred_element_type=F32)
        for y_ in range(4):
            ds[pair, y_] = acc[:, y_ * 128 : (y_ + 1) * 128].astype(BF16)
        for o in (1, 3, 2):
            send = remote(
                ds.at[pair, rem(y + o, 4)], dyr.at[u, y], dy_send + pair * 3 + o - 1,
                dy_recv + u * 4 + y, around_y[o - 1],
            )
            send.start()
            pending.append(send)
        dyr[u, y] = ds[pair, y]

    def write_panel(step, c_copy):
        c_copy.wait_recv()
        mine = pb[step, pl.ds(pl.multiple_of(k * 64, 64), 64)]
        res = jnp.dot(mine, perm[k], preferred_element_type=F32)
        res += jnp.dot(cr[step], perm[1 - k], preferred_element_type=F32)
        for s in range(2):
            lane = (2 * u_of[step] + s) * 512 + zh_at[step % 2] * 256
            panel_ref[:, pl.ds(pl.multiple_of(lane, 256), 256)] = res[
                :, s * 256 : (s + 1) * 256
            ].astype(BF16)

    neighbours(0)
    loads[4].wait()
    a_theirs.wait_recv()
    partial(0)
    send_y(0)
    neighbours(1)
    partial(1)
    send_y(1)
    z0 = reduce_y(0)

    fr_mine.wait()
    for copy in fr_arrive:
        copy.wait_recv()
    fr_sems = take(2)
    fr_swap = remote(fr.at[:, :, k], fr.at[:, :, k], fr_sems, fr_sems + 1, partner)
    fr_swap.start()
    pending.append(fr_swap)

    far(0)
    partial(2)
    send_y(2)
    z1 = reduce_y(1)
    c0 = finish(0, z0)
    far(1)
    partial(3)
    send_y(3)
    z2 = reduce_y(2)
    c1 = finish(1, z1)
    remote(fr.at[:, :, 1 - k], fr.at[:, :, 1 - k], fr_sems, fr_sems + 1, partner).wait_recv()
    products(0)
    z3 = reduce_y(3)
    write_panel(0, c0)
    write_panel(1, c1)
    c2 = finish(2, z2)
    c3 = finish(3, z3)
    products(1)
    write_panel(2, c2)
    write_panel(3, c3)

    def over_y(u):
        for o in (1, 3, 2):
            y_from = rem(y + o, 4)
            remote(
                ds.at[0, 0], dyr.at[u, y_from], dy_send, dy_recv + u * 4 + y_from,
                around_y[o - 1],
            ).wait_recv()
        for zl_ in range(4):
            rows = slice(zl_ * 128, (zl_ + 1) * 128)
            acc = dyr[u, 0, rows].astype(F32)
            for y_ in range(1, 4):
                acc += dyr[u, y_, rows].astype(F32)
            for x_ in range(4):
                dxs[x_, u, zl_] = acc[x_ * 32 : (x_ + 1) * 32].astype(BF16)

    over_y(u_own)
    over_y(1 - u_own)
    arrive = []
    for o in (1, 3, 2):
        send, recv = take(), take()
        copy = remote(dxs.at[rem(x + o, 4)], dxr.at[o - 1], send, recv, around_x[o - 1])
        copy.start()
        pending.append(copy)
        arrive.append(remote(dxs.at[x], dxr.at[o - 1], send, recv, around_x[3 - o]))
    for copy in arrive:
        copy.wait_recv()
    acc = dxs[x].astype(F32)
    for o in range(3):
        acc += dxr[o].astype(F32)
    for zl_ in range(4):
        dzs[zl_] = acc[:, zl_].astype(BF16)
    arrive = []
    for o in (4, 3, 5, 2, 6, 1, 7):
        z_to, z_from = rem(z + o, 8), rem(z + 8 - o, 8)
        send, recv = take(), take()
        copy = remote(dzs.at[rem(z_to, 4)], dzr.at[o - 1], send, recv, chip_z(z_to))
        copy.start()
        pending.append(copy)
        arrive.append(remote(dzs.at[zl], dzr.at[o - 1], send, recv, chip_z(z_from)))
    for copy in arrive:
        copy.wait_recv()
    total = dzs[zl].astype(F32)
    for o in range(7):
        total += dzr[o].astype(F32)
    total = jnp.where(zh == 0, total[:, :, :64], total[:, :, 64:])
    loads[3].wait()
    for s in range(4):
        diag_ref[s] = inv_ref[s] - total[s // 2, :, (s % 2) * 32 : (s % 2 + 1) * 32]

    for copy in pending:
        if isinstance(copy, tuple):
            sent, copy = copy
            pl.when(sent)(copy.wait_send)
        else:
            copy.wait_send()
    assert used[0] <= SEMS, used


SEMS = 208


def per_device(inverse_tiles, factor, inverse_diag, tile_list, tile_count):
    vmem = pl.BlockSpec(memory_space=pltpu.VMEM)
    v = pltpu.VMEM
    panel, diag = pl.pallas_call(
        kernel,
        out_shape=(
            jax.ShapeDtypeStruct((64, 2048), BF16),
            jax.ShapeDtypeStruct((4, 32, 32), F32),
        ),
        in_specs=[pl.BlockSpec(memory_space=pl.ANY)] * 5,
        out_specs=(vmem, vmem),
        scratch_shapes=[
            v((4, 128), jnp.int32),
            pltpu.SMEM((4,), jnp.int32),
            v((4, 32, 1024), BF16),
            v((4, 32, 32), F32),
            v((2, 1024, 1024), BF16),
            v((4, 32, 1024), BF16),
            v((8, 4, 32, 128), BF16),
            v((4, 2, 2, 32, 1024), BF16),
            v((4, 2, 4, 2, 32, 1024), BF16),
            v((4, 8, 2, 32, 128), BF16),
            v((4, 2, 4, 128, 256), BF16),
            v((4, 3, 2, 128, 256), BF16),
            v((4, 128, 256), F32),
            v((4, 128, 256), BF16),
            v((4, 128, 256), BF16),
            v((4, 128, 256), BF16),
            v((4, 64, 256), BF16),
            v((2, 4, 512, 128), BF16),
            v((2, 4, 512, 128), BF16),
            v((4, 2, 4, 32, 128), BF16),
            v((3, 2, 4, 32, 128), BF16),
            v((4, 2, 32, 128), BF16),
            v((7, 2, 32, 128), BF16),
            v((2, 256, 512), BF16),
            v((2, 256, 512), BF16),
            pltpu.SemaphoreType.DMA((SEMS,)),
        ],
        compiler_params=pltpu.CompilerParams(
            collective_id=0, has_side_effects=True, vmem_limit_bytes=60 * 1024 * 1024
        ),
        cost_estimate=pl.CostEstimate(
            flops=2 * 1024 * 2048 * 1024, bytes_accessed=4 << 20, transcendentals=0
        ),
    )(tile_list, tile_count, inverse_tiles, jnp.transpose(factor, (1, 2, 0)), inverse_diag)
    return panel.reshape(64, 4, 512), diag


def solution(mesh):
    return jax.shard_map(
        per_device,
        mesh=mesh,
        in_specs=(P("row", "col"), P("row", None, "col"), P(None, "row", "col"), P(), P()),
        out_specs=(P(("row", "col"), None, None), P(None, "row", "col")),
        check_vma=False,
    )
```

time: 154 us -> 119 us (0.77); the launches traced: 151 us -> 119 us
  Pallas kernels: 144 us -> 115 us
  local copies, waits for them, and re-layouts: 6.22 us -> 3.31 us
    pallas_call x1, Pallas kernels: 144 us -> 115 us  [per_device(): pl.pallas_call(kernel, out_shape=(jax.ShapeDtypeStruct((64, 2048), BF16),...]
    unnamed x11 -> x1, local copies, waits for them, and re-layouts: 5.34 us -> 1.47 us
where the time goes in v2:
time: 119 us
  Pallas kernels  115 us (97%)
  local copies, waits for them, and re-layouts  3.31 us (3%)
    pallas_call x1, Pallas kernels, per_device(): pl.pallas_call(kernel, out_shape=(jax.ShapeDtypeStruct((64, 2048), BF16),...  115 us

profile of v2, /device:TPU:32, one launch (start us, length us, event | category | flops | bytes accessed | tf_op | source)
XLA Modules:
  0.0 118.7 jit_solution(2466439916032364390)
XLA Ops:
  0.6 114.8 %shard_map.68 = (bf16[64,2048]{1,0:T(8,128)(2,1)}, f32[4,32,32]{2,1,0:T(8,128)}) custom-call(s32[4,128]{1,0:T(4,128)} %list_hbm.1, s32[4]{0:T(128)} %count_hbm.1, bf16[1024,1024]{1,0:T(8,128)(2,1)} %a_ref.1, bf16[4,32,1024]{2,1,0:T(8,128)(2,1)} %bitcast.1, f32[4,32,32]{2,1,0:T(8,128)} %inv_hbm.1), custom_call_target="tpu_custom_call" | custom-call | flops 4294967296 | bytes 4194304 | tf_op jit(solution)/shard_map/pallas_call | solution.py:481
  115.4 1.8 %reshape.7 = bf16[64,4,512]{2,1,0:T(4,128)(2,1)} reshape(bf16[64,2048]{1,0:T(8,128)(2,1)} %get-tuple-element.4) | data formatting | bytes 524288 | tf_op jit(solution)/shard_map/reshape | solution.py:524
  117.3 1.5 %copy.8 = f32[4,32,32]{2,1,0:T(8,128)} copy(f32[4,32,32]{2,1,0:T(8,128)} %get-tuple-element.9) | data formatting | bytes 32768

commit v3 on v2

--- a/solution.py
+++ b/solution.py
@@ -22,7 +22,7 @@
 def kernel(
     list_hbm, count_hbm, a_ref, ft_hbm, inv_hbm, panel_ref, diag_ref,
     list_ref, count_ref, ft_ref, inv_ref,
-    abuf, fmask, ftile, zbuf, fg, fr, pp, pyr, zown, zs, zr, pb, cr, ds, dyr, dxs, dxr, dzs, dzr,
+    abuf, fmask, ftile, fg, fr, pp, pyr, zown, zs, zr, pb, cr, ds, dyr, dxs, dxr, dzs, dzr,
     perm, spread, sems,
 ):
     row, col = lax.axis_index("row"), lax.axis_index("col")
@@ -56,10 +56,16 @@
     def chip_z(z_, x_=x):
         return at(zh_=div(z_, 4), zl_=rem(z_, 4), x_=x_)
 
-    swap_z = jnp.where((z >= 2) & (z <= 5), 7 - z, z)
-    moves = swap_z != z
-    across = chip_z(swap_z, rem(x + 2, 4))
-    u_own, h_own = div(x, 2), rem(x, 2)
+    u_own = div(x, 2)
+    to_zh, to_y = div(zl, 2), rem(zl, 2) * 2 + div(x, 2)
+    to_place, to_yh = zh * 2 + rem(y, 2), div(y, 2)
+    here = (to_zh == zh) & (to_y == y) & (to_place == zl)
+
+    def source(yh):
+        return at(
+            x_=jnp.where(u_own == rem(y, 2), x, rem(x + 2, 4)), y_=yh * 2 + rem(zl, 2),
+            zh_=div(zl, 2), zl_=zh * 2 + div(y, 2),
+        )
 
     first = take(5)
     loads = [
@@ -86,9 +92,12 @@
         if o != 4:
             greet(chip_z(rem(z + o, 8)))
 
-    @pl.when(moves)
-    def _():
-        greet(across)
+    for yh in range(2):
+        s_row, s_col = source(yh)
+
+        @pl.when((s_row != row) | (s_col != col))
+        def _():
+            greet((s_row, s_col))
 
     for copy in loads[:3]:
         copy.wait()
@@ -113,29 +122,35 @@
             ftile[i, s] = block
     alive = live(row * 8 + t)
 
-    pl.semaphore_wait(barrier, 17 + jnp.where(moves, 1, 0))
+    pl.semaphore_wait(barrier, 19 - jnp.where(here, 1, 0))
 
     pending = []
 
     hop_send, hop_recv = take(2), take(2)
     kept = fmask.at[pl.ds(u_own * 2, 2)]
     given = fmask.at[pl.ds((1 - u_own) * 2, 2)]
-    zl_there = rem(swap_z, 4)
-    local_kept = pltpu.make_async_copy(kept, zbuf.at[zl, u_own], sems.at[hop_recv])
-    remote_kept = remote(kept, zbuf.at[zl_there, u_own], hop_send, hop_recv, chip_z(swap_z))
-
-    @pl.when(moves)
+    across = rem(x + 2, 4)
+    gift = remote(
+        given, fg.at[across, to_place, to_yh], hop_send + 1, hop_recv + to_yh,
+        at(x_=across, y_=to_y, zh_=to_zh, zl_=to_place),
+    )
+    gift.start()
+    pending.append(gift)
+    there = fg.at[x, to_place, to_yh]
+    local_kept = pltpu.make_async_copy(kept, there, sems.at[hop_recv + to_yh])
+    remote_kept = remote(
+        kept, there, hop_send, hop_recv + to_yh, at(y_=to_y, zh_=to_zh, zl_=to_place)
+    )
+
+    @pl.when(here)
+    def _():
+        local_kept.start()
+
+    @pl.when(jnp.logical_not(here))
     def _():
         remote_kept.start()
 
-    @pl.when(jnp.logical_not(moves))
-    def _():
-        local_kept.start()
-
-    pending.append((moves, remote_kept))
-    gift = remote(given, zbuf.at[zl_there, u_own], hop_send + 1, hop_recv + 1, across)
-    gift.start()
-    pending.append(gift)
+    pending.append((jnp.logical_not(here), remote_kept))
 
     a_sems = take(2)
     a_swap = remote(a_ref, abuf.at[k], a_sems, a_sems + 1, partner)
@@ -143,32 +158,10 @@
     pending.append(a_swap)
     a_theirs = remote(a_ref, abuf.at[1 - k], a_sems, a_sems + 1, partner)
 
-    line_send, line_recv = take(6), take(6)
-
-    def held(i):
-        if i == 0:
-            return zl
-        if i == 1:
-            return zl + 1 - 2 * rem(zl, 2)
-        if i == 2:
-            return rem(zl + 2, 4)
-        return 3 - zl
-
-    remote(kept, zbuf.at[zl, u_own], hop_send, hop_recv, chip_z(swap_z)).wait_recv()
-    remote(given, zbuf.at[zl, 1 - u_own], hop_send + 1, hop_recv + 1, across).wait_recv()
-    for i in (1, 2, 3):
-        for b in range(2):
-            sem = (i - 1) * 2 + b
-            copy = remote(
-                zbuf.at[zl, b], zbuf.at[zl, b], line_send + sem, line_recv + sem,
-                at(zl_=held(i)),
-            )
-            copy.start()
-            pending.append(copy)
-
     r_iota = lax.broadcasted_iota(jnp.int32, (256, 512), 0)
     c_iota = lax.broadcasted_iota(jnp.int32, (256, 512), 1)
-    r_y, r_s, r_w = div(r_iota, 64), rem(div(r_iota, 32), 2), rem(r_iota, 32)
+    r_y = rem(div(r_iota, 64), 2) * 2 + div(r_iota, 128)
+    r_s, r_w = rem(div(r_iota, 32), 2), rem(r_iota, 32)
     same_w = r_w == rem(c_iota, 32)
     for core in range(2):
         hit = same_w & (r_s == div(c_iota, 256)) & (div(rem(c_iota, 256), 32) == r_y * 2 + core)
@@ -177,47 +170,45 @@
         hit = same_w & (r_y == div(c_iota, 128)) & (div(rem(c_iota, 128), 32) == half * 2 + r_s)
         spread[half] = jnp.where(hit, 1.0, 0.0).astype(BF16)
 
-    y_send, y_recv = take(8), take(8)
-    right_send, right_recv, left_send, left_recv = take(8), take(8), take(8), take(8)
+    line_send, line_recv, pass_send = take(2), take(4), take(3)
+    right_send, right_recv, left_send, left_recv = take(4), take(4), take(4), take(4)
     zh_at = [div(zl, 2), 1 - div(zl, 2)]
-    for q in range(2):
-        for i in (2 * q, 2 * q + 1):
-            place = held(i)
-            z_from = zh * 4 + place
-            z_from = jnp.where((z_from >= 2) & (z_from <= 5), 7 - z_from, z_from)
-            for b in range(2):
-                block = zbuf.at[place, b]
-                if i > 0:
-                    sem = (i - 1) * 2 + b
-                    remote(
-                        block, block, line_send + sem, line_recv + sem, at(zl_=place)
-                    ).wait_recv()
-                y_to = rem(z_from, 2) * 2 + b
-                there = fg.at[x, zh_at[q], y]
-                sem = y_recv + q * 4 + y
-                stay = pltpu.make_async_copy(block, there, sems.at[sem])
-                send = remote(block, there, y_send + i * 2 + b, sem, at(y_=y_to))
-
-                @pl.when(y_to == y)
-                def _():
-                    stay.start()
-
-                @pl.when(y_to != y)
-                def _():
-                    send.start()
-
-                pending.append((y_to != y, send))
-        for o in (0, 1, 3, 2):
-            y_from = rem(y + o, 4)
-            block = fg.at[x, zh_at[q], y_from]
-            sem = q * 4 + y_from
-            remote(block, block, y_send, y_recv + sem, around_y[o - 1]).wait_recv()
-            for send, recv, device in (
-                (right_send, right_recv, right), (left_send, left_recv, left)
-            ):
-                copy = remote(block, block, send + sem, recv + sem, device)
-                copy.start()
-                pending.append(copy)
+    inner = (zl == 1) | (zl == 2)
+    even = rem(zl, 2) == 0
+    flip1 = jnp.where(even, zl + 1, zl - 1)
+    flip2 = rem(zl + 2, 4)
+    flip3 = 3 - zl
+    order = [zl, flip1, jnp.where(inner, flip3, flip2), jnp.where(inner, flip2, flip3)]
+
+    def along_line(place, sem, to):
+        on = (to >= 0) & (to <= 3)
+        block = fg.at[x, place]
+        copy = remote(block, block, sem, line_recv + place, at(zl_=jnp.clip(to, 0, 3)))
+        pl.when(on)(copy.start)
+        pending.append((on, copy))
+
+    def along_x(place):
+        block = fg.at[x, place]
+        for send, recv, device in (
+            (right_send, right_recv, right), (left_send, left_recv, left)
+        ):
+            copy = remote(block, block, send + place, recv + place, device)
+            copy.start()
+            pending.append(copy)
+
+    for yh in range(2):
+        remote(
+            kept, fg.at[x, zl, yh], hop_send, hop_recv + yh, around_x[0]
+        ).wait_recv()
+    along_line(zl, line_send, zl + 1)
+    along_line(zl, line_send + 1, zl - 1)
+    along_x(zl)
+    for i in (1, 2, 3):
+        place = order[i]
+        block = fg.at[x, place]
+        remote(block, block, line_send, line_recv + place, around_x[0]).wait_recv()
+        along_line(place, pass_send + i - 1, jnp.where(place > zl, zl - 1, zl + 1))
+        along_x(place)
 
     fr_own_sem = take()
     fr_mine = pltpu.make_async_copy(ftile.at[t], fr.at[:, t, k], sems.at[fr_own_sem])
@@ -235,41 +226,25 @@
     far_right_send, far_right_recv = take(4), take(4)
     far_left_send, far_left_recv = take(4), take(4)
 
-    def from_left(q, y_):
-        block = fg.at[g_left, zh_at[q], y_]
-        sem = q * 4 + y_
-        remote(block, block, right_send + sem, right_recv + sem, left).wait_recv()
-        if y_ < 2:
-            sem = q * 2 + y_
-            copy = remote(block, block, far_right_send + sem, far_right_recv + sem, right)
+    def neighbours(i):
+        place = order[i]
+        for sems_at, group, half, onward, device, back in (
+            ((right_send, right_recv), g_left, 0, (far_right_send, far_right_recv), right, left),
+            ((left_send, left_recv), g_right, 1, (far_left_send, far_left_recv), left, right),
+        ):
+            block = fg.at[group, place]
+            remote(block, block, sems_at[0] + place, sems_at[1] + place, back).wait_recv()
+            part = fg.at[group, place, half]
+            copy = remote(part, part, onward[0] + place, onward[1] + place, device)
             copy.start()
             pending.append(copy)
 
-    def from_right(q, y_):
-        block = fg.at[g_right, zh_at[q], y_]
-        sem = q * 4 + y_
-        remote(block, block, left_send + sem, left_recv + sem, right).wait_recv()
-        if y_ >= 2:
-            sem = q * 2 + y_ - 2
-            copy = remote(block, block, far_left_send + sem, far_left_recv + sem, left)
-            copy.start()
-            pending.append(copy)
-
-    def neighbours(q):
-        for y_ in range(2):
-            from_left(q, y_)
-            from_right(q, y_ + 2)
-        for y_ in range(2):
-            from_left(q, y_ + 2)
-            from_right(q, y_)
-
-    def far(q):
-        for y_ in range(2):
-            sem = q * 2 + y_
-            block = fg.at[g_far, zh_at[q], y_]
-            remote(block, block, far_right_send + sem, far_right_recv + sem, left).wait_recv()
-            block = fg.at[g_far, zh_at[q], y_ + 2]
-            remote(block, block, far_left_send + sem, far_left_recv + sem, right).wait_recv()
+    def far(i):
+        place = order[i]
+        part = fg.at[g_far, place, 0]
+        remote(part, part, far_right_send, far_right_recv + place, left).wait_recv()
+        part = fg.at[g_far, place, 1]
+        remote(part, part, far_left_send, far_left_recv + place, right).wait_recv()
 
     u_of = [u_own, u_own, 1 - u_own, 1 - u_own]
 
@@ -279,11 +254,11 @@
         def body(i, carry):
             rows = pl.ds(pl.multiple_of(i * 256, 256), 256)
             acc = lax.dot_general(
-                abuf[0, rows], fg[2 * u, half].reshape(256, 1024), NT_DIMS,
+                abuf[0, rows], fg[2 * u, pl.ds(2 * half, 2)].reshape(256, 1024), NT_DIMS,
                 preferred_element_type=F32,
             )
             acc += lax.dot_general(
-                abuf[1, rows], fg[2 * u + 1, half].reshape(256, 1024), NT_DIMS,
+                abuf[1, rows], fg[2 * u + 1, pl.ds(2 * half, 2)].reshape(256, 1024), NT_DIMS,
                 preferred_element_type=F32,
             )
             first = rem(i, 2) * 2
@@ -376,15 +351,12 @@
             ].astype(BF16)
 
     neighbours(0)
+    neighbours(1)
     loads[4].wait()
     a_theirs.wait_recv()
     partial(0)
     send_y(0)
-    neighbours(1)
-    partial(1)
-    send_y(1)
-    z0 = reduce_y(0)
-
+    neighbours(2)
     fr_mine.wait()
     for copy in fr_arrive:
         copy.wait_recv()
@@ -392,26 +364,31 @@
     fr_swap = remote(fr.at[:, :, k], fr.at[:, :, k], fr_sems, fr_sems + 1, partner)
     fr_swap.start()
     pending.append(fr_swap)
-
+    z0 = reduce_y(0)
+    neighbours(3)
+    partial(1)
+    send_y(1)
     far(0)
+    far(1)
     partial(2)
     send_y(2)
     z1 = reduce_y(1)
     c0 = finish(0, z0)
-    far(1)
+    remote(fr.at[:, :, 1 - k], fr.at[:, :, 1 - k], fr_sems, fr_sems + 1, partner).wait_recv()
+    c1 = finish(1, z1)
+    products(0)
+    z2 = reduce_y(2)
+    far(2)
+    far(3)
     partial(3)
     send_y(3)
-    z2 = reduce_y(2)
-    c1 = finish(1, z1)
-    remote(fr.at[:, :, 1 - k], fr.at[:, :, 1 - k], fr_sems, fr_sems + 1, partner).wait_recv()
-    products(0)
-    z3 = reduce_y(3)
     write_panel(0, c0)
     write_panel(1, c1)
     c2 = finish(2, z2)
+    z3 = reduce_y(3)
+    write_panel(2, c2)
     c3 = finish(3, z3)
     products(1)
-    write_panel(2, c2)
     write_panel(3, c3)
 
     def over_y(u):
@@ -494,8 +471,7 @@
             v((2, 1024, 1024), BF16),
             v((4, 32, 1024), BF16),
             v((8, 4, 32, 128), BF16),
-            v((4, 2, 2, 32, 1024), BF16),
-            v((4, 2, 4, 2, 32, 1024), BF16),
+            v((4, 4, 2, 2, 32, 1024), BF16),
             v((4, 8, 2, 32, 128), BF16),
             v((4, 2, 4, 128, 256), BF16),
             v((4, 3, 2, 128, 256), BF16),

time: 119 us -> 110 us (0.924)
  Pallas kernels: 115 us -> 106 us
    pallas_call x1, Pallas kernels: 115 us -> 106 us  [per_device(): pl.pallas_call(kernel, out_shape=(jax.ShapeDtypeStruct((64, 2048), BF16),...]
where the time goes in v3:
time: 110 us
  Pallas kernels  106 us (96%)
  local copies, waits for them, and re-layouts  3.31 us (3%)
    pallas_call x1, Pallas kernels, per_device(): pl.pallas_call(kernel, out_shape=(jax.ShapeDtypeStruct((64, 2048), BF16),...  106 us

profile of v3, /device:TPU:32, one launch (start us, length us, event | category | flops | bytes accessed | tf_op | source)
XLA Modules:
  0.0 109.8 jit_solution(8690221161830861745)
XLA Ops:
  0.6 105.8 %shard_map.68 = (bf16[64,2048]{1,0:T(8,128)(2,1)}, f32[4,32,32]{2,1,0:T(8,128)}) custom-call(s32[4,128]{1,0:T(4,128)} %list_hbm.1, s32[4]{0:T(128)} %count_hbm.1, bf16[1024,1024]{1,0:T(8,128)(2,1)} %a_ref.1, bf16[4,32,1024]{2,1,0:T(8,128)(2,1)} %bitcast.1, f32[4,32,32]{2,1,0:T(8,128)} %inv_hbm.1), custom_call_target="tpu_custom_call" | custom-call | flops 4294967296 | bytes 4194304 | tf_op jit(solution)/shard_map/pallas_call | solution.py:458
  106.5 1.8 %reshape.7 = bf16[64,4,512]{2,1,0:T(4,128)(2,1)} reshape(bf16[64,2048]{1,0:T(8,128)(2,1)} %get-tuple-element.4) | data formatting | bytes 524288 | tf_op jit(solution)/shard_map/reshape | solution.py:500
  108.3 1.5 %copy.8 = f32[4,32,32]{2,1,0:T(8,128)} copy(f32[4,32,32]{2,1,0:T(8,128)} %get-tuple-element.9) | data formatting | bytes 32768

commit v4 on v3

--- a/solution.py
+++ b/solution.py
@@ -22,8 +22,8 @@
 def kernel(
     list_hbm, count_hbm, a_ref, ft_hbm, inv_hbm, panel_ref, diag_ref,
     list_ref, count_ref, ft_ref, inv_ref,
-    abuf, fmask, ftile, fg, fr, pp, pyr, zown, zs, zr, pb, cr, ds, dyr, dxs, dxr, dzs, dzr,
-    perm, spread, sems,
+    abuf, fmask, ftile, fg, fr, pp, pyr, sb, zown, zs, zr, pb, cr, ds, dyr, dxs, dxr, dzs,
+    dzr, perm, sems,
 ):
     row, col = lax.axis_index("row"), lax.axis_index("col")
     zl, x = div(row, 4), rem(row, 4)
@@ -119,8 +119,8 @@
             keep = jnp.broadcast_to(alive[s : s + 1, :], block.shape) > 0
             block = jnp.where(keep, block.astype(F32), 0.0).astype(BF16)
             fmask[s, :, i * 128 : (i + 1) * 128] = block
-            ftile[i, s] = block
-    alive = live(row * 8 + t)
+            ftile[i % 4, s, :, (i // 4) * 128 : (i // 4 + 1) * 128] = block
+    alive = [live(row * 8 + half * 4 + y) for half in range(2)]
 
     pl.semaphore_wait(barrier, 19 - jnp.where(here, 1, 0))
 
@@ -166,10 +166,6 @@
     for core in range(2):
         hit = same_w & (r_s == div(c_iota, 256)) & (div(rem(c_iota, 256), 32) == r_y * 2 + core)
         perm[core] = jnp.where(hit, 1.0, 0.0).astype(BF16)
-    for half in range(2):
-        hit = same_w & (r_y == div(c_iota, 128)) & (div(rem(c_iota, 128), 32) == half * 2 + r_s)
-        spread[half] = jnp.where(hit, 1.0, 0.0).astype(BF16)
-
     line_send, line_recv, pass_send = take(2), take(4), take(3)
     right_send, right_recv, left_send, left_recv = take(4), take(4), take(4), take(4)
     zh_at = [div(zl, 2), 1 - div(zl, 2)]
@@ -203,7 +199,7 @@
     along_line(zl, line_send, zl + 1)
     along_line(zl, line_send + 1, zl - 1)
     along_x(zl)
-    for i in (1, 2, 3):
+    def arrive_z(i):
         place = order[i]
         block = fg.at[x, place]
         remote(block, block, line_send, line_recv + place, around_x[0]).wait_recv()
@@ -211,16 +207,20 @@
         along_x(place)
 
     fr_own_sem = take()
-    fr_mine = pltpu.make_async_copy(ftile.at[t], fr.at[:, t, k], sems.at[fr_own_sem])
+    fr_mine = pltpu.make_async_copy(ftile.at[y], fr.at[:, t, k], sems.at[fr_own_sem])
     fr_mine.start()
     fr_arrive = []
-    for o in range(1, 8):
-        t_to, t_from = rem(t + o, 8), rem(t + 8 - o, 8)
-        send, recv = take(), take()
-        copy = remote(ftile.at[t_to], fr.at[:, t, k], send, recv, chip_t(t_to))
-        copy.start()
-        pending.append(copy)
-        fr_arrive.append(remote(ftile.at[t], fr.at[:, t_from, k], send, recv, chip_t(t_from)))
+
+    def share_rows():
+        for o in range(1, 8):
+            t_to, t_from = rem(t + o, 8), rem(t + 8 - o, 8)
+            send, recv = take(), take()
+            copy = remote(ftile.at[rem(t_to, 4)], fr.at[:, t, k], send, recv, chip_t(t_to))
+            copy.start()
+            pending.append(copy)
+            fr_arrive.append(
+                remote(ftile.at[y], fr.at[:, t_from, k], send, recv, chip_t(t_from))
+            )
 
     g_left, g_right, g_far = rem(x + 3, 4), rem(x + 1, 4), rem(x + 2, 4)
     far_right_send, far_right_recv = take(4), take(4)
@@ -246,98 +246,90 @@
         part = fg.at[g_far, place, 1]
         remote(part, part, far_left_send, far_left_recv + place, right).wait_recv()
 
-    u_of = [u_own, u_own, 1 - u_own, 1 - u_own]
-
-    def partial(step):
-        u, half = u_of[step], zh_at[step % 2]
-
-        def body(i, carry):
-            rows = pl.ds(pl.multiple_of(i * 256, 256), 256)
+    u_of = [u_own, 1 - u_own]
+    b_of = [rem(place, 2) for place in order]
+
+    def partial(i, w):
+        u, place, c = u_of[w], order[i], i * 2 + w
+
+        def body(n, carry):
+            rows = pl.ds(pl.multiple_of(n * 256, 256), 256)
             acc = lax.dot_general(
-                abuf[0, rows], fg[2 * u, pl.ds(2 * half, 2)].reshape(256, 1024), NT_DIMS,
+                abuf[0, rows], fg[2 * u, place].reshape(128, 1024), NT_DIMS,
                 preferred_element_type=F32,
             )
             acc += lax.dot_general(
-                abuf[1, rows], fg[2 * u + 1, pl.ds(2 * half, 2)].reshape(256, 1024), NT_DIMS,
+                abuf[1, rows], fg[2 * u + 1, place].reshape(128, 1024), NT_DIMS,
                 preferred_element_type=F32,
             )
-            first = rem(i, 2) * 2
+            first = rem(n, 2) * 2
             for j in range(2):
-                pp[step, div(i, 2), first + j] = acc[j * 128 : (j + 1) * 128].astype(BF16)
+                pp[c, div(n, 2), first + j] = acc[j * 128 : (j + 1) * 128].astype(BF16)
             return carry
 
         lax.fori_loop(0, 4, body, 0)
-
-    y_sems = take(24)
-    z_sems, c_sems = take(8), take(8)
-    dy_send, dy_recv = take(6), take(8)
-
-    def send_y(step):
-        for o in (1, 2, 3):
-            sem = y_sems + (step * 3 + o - 1) * 2
+        for o in (2, 1, 3):
+            sem = y_sems + (c * 3 + o - 1) * 2
             copy = remote(
-                pp.at[step, :, rem(y + o, 4)], pyr.at[step, o - 1], sem, sem + 1, around_y[o - 1]
+                pp.at[c, :, rem(y + o, 4)], pyr.at[c, o - 1], sem, sem + 1, around_y[o - 1]
             )
             copy.start()
             pending.append(copy)
 
-    def reduce_y(step):
-        for o in (1, 2, 3):
-            sem = y_sems + (step * 3 + o - 1) * 2
+    y_sems = take(48)
+    z_sems, c_sems = take(8), take(8)
+    dy_send, dy_recv = take(8), take(8)
+    dx_sems = take(12)
+    dz_send, dz_recv = take(8), take(8)
+
+    lane = lax.broadcasted_iota(jnp.int32, (1, 128), 1)
+    lane_s = rem(div(lane, 32), 2)
+    low = jnp.broadcast_to(lane, (512, 128)) < 64
+    lane_live = []
+    for w in range(2):
+        for half in range(2):
+            mask = jnp.zeros((1, 128), F32)
+            for s in range(4):
+                mask = jnp.where(lane_s + 2 * u_of[w] == s, alive[half][s : s + 1, :], mask)
+            lane_live.append(mask)
+
+    def reduce_y(i, w):
+        c, step = i * 2 + w, w * 2 + i // 2
+        for o in (1, 3, 2):
+            sem = y_sems + (c * 3 + o - 1) * 2
             came = around_y[3 - o]
-            remote(pp.at[step, :, y], pyr.at[step, o - 1], sem, sem + 1, came).wait_recv()
-
-        def total(which):
-            acc = pp[step, which, y].astype(F32)
+            remote(pp.at[c, :, y], pyr.at[c, o - 1], sem, sem + 1, came).wait_recv()
+        sums = []
+        for half in range(2):
+            acc = pp[c, half, y].astype(F32)
             for o in range(3):
-                acc += pyr[step, o, which].astype(F32)
-            return acc
-
-        zs[step] = total(1 - zh).astype(BF16)
+                acc += pyr[c, o, half].astype(F32)
+            acc = jnp.where(lane_live[w * 2 + half] > 0, acc, 0.0)
+            for s in range(2):
+                sb[i, u_of[w], s, half * 128 : (half + 1) * 128] = jnp.where(
+                    lane_s == s, acc, 0.0
+                ).astype(BF16)
+            sums.append(acc)
+        lanes = pl.ds(pl.multiple_of(b_of[i] * 128, 128), 128)
+        zown[step, :, lanes] = jnp.where(zh == 0, sums[0], sums[1])
+        zs[step, :, lanes] = jnp.where(zh == 0, sums[1], sums[0]).astype(BF16)
+
+    def exchange(step):
         copy = remote(
             zs.at[step], zr.at[step], z_sems + step * 2, z_sems + step * 2 + 1, at(zh_=1 - zh)
         )
         copy.start()
         pending.append(copy)
-        zown[step] = total(zh)
         return copy
-
-    lane_s = rem(div(lax.broadcasted_iota(jnp.int32, (1, 256), 1), 32), 2)
-    wide_s = rem(div(lax.broadcasted_iota(jnp.int32, (1, 512), 1), 32), 2)
 
     def finish(step, z_copy):
         z_copy.wait_recv()
-        s_here = lane_s + 2 * u_of[step]
-        lane_live = jnp.zeros((1, 256), F32)
-        for s in range(4):
-            lane_live = jnp.where(s_here == s, alive[s : s + 1, :], lane_live)
-        panel = -(zown[step] + zr[step].astype(F32))
-        panel = jnp.where(lane_live > 0, panel, 0.0)
-        pb[step] = panel.astype(BF16)
+        pb[step] = (-(zown[step] + zr[step].astype(F32))).astype(BF16)
         theirs = pb.at[step, pl.ds(pl.multiple_of((1 - k) * 64, 64), 64)]
         copy = remote(theirs, cr.at[step], c_sems + step * 2, c_sems + step * 2 + 1, partner)
         copy.start()
         pending.append(copy)
         return copy
-
-    def products(pair):
-        step, u = pair * 2, u_of[pair * 2]
-        panel = jnp.dot(pb[step], spread[zh_at[0]], preferred_element_type=F32)
-        panel += jnp.dot(pb[step + 1], spread[zh_at[1]], preferred_element_type=F32)
-        acc = jnp.zeros((512, 512), F32)
-        for s in range(2):
-            part = jnp.where(wide_s == s, panel, 0.0).astype(BF16)
-            acc += jnp.dot(fr[2 * u + s].reshape(512, 128), part, preferred_element_type=F32)
-        for y_ in range(4):
-            ds[pair, y_] = acc[:, y_ * 128 : (y_ + 1) * 128].astype(BF16)
-        for o in (1, 3, 2):
-            send = remote(
-                ds.at[pair, rem(y + o, 4)], dyr.at[u, y], dy_send + pair * 3 + o - 1,
-                dy_recv + u * 4 + y, around_y[o - 1],
-            )
-            send.start()
-            pending.append(send)
-        dyr[u, y] = ds[pair, y]
 
     def write_panel(step, c_copy):
         c_copy.wait_recv()
@@ -345,18 +337,108 @@
         res = jnp.dot(mine, perm[k], preferred_element_type=F32)
         res += jnp.dot(cr[step], perm[1 - k], preferred_element_type=F32)
         for s in range(2):
-            lane = (2 * u_of[step] + s) * 512 + zh_at[step % 2] * 256
-            panel_ref[:, pl.ds(pl.multiple_of(lane, 256), 256)] = res[
+            at_lane = (2 * u_of[step // 2] + s) * 512 + zh_at[step % 2] * 256
+            panel_ref[:, pl.ds(pl.multiple_of(at_lane, 256), 256)] = res[
                 :, s * 256 : (s + 1) * 256
             ].astype(BF16)
 
+    def products(i):
+        both = []
+        for u in range(2):
+            acc = jnp.zeros((512, 128), F32)
+            for s in range(2):
+                acc += jnp.dot(
+                    fr[2 * u + s].reshape(512, 256), sb[i, u, s], preferred_element_type=F32
+                )
+            both.append(acc)
+        turned = [pltpu.roll(acc, 64, 1) for acc in both]
+        ds[i, 0] = jnp.where(low, both[0], turned[1]).astype(BF16)
+        ds[i, 1] = jnp.where(low, turned[0], both[1]).astype(BF16)
+        half = zh_at[i // 2]
+        for yh in range(2):
+            y_to = yh * 2 + b_of[i]
+            send = remote(
+                ds.at[i, yh], dyr.at[half, y], dy_send + i * 2 + yh, dy_recv + half * 4 + y,
+                at(y_=y_to),
+            )
+            pl.when(y_to != y)(send.start)
+            pending.append((y_to != y, send))
+
+            @pl.when(y_to == y)
+            def _():
+                dyr[half, y] = ds[i, yh]
+
+    def over_y(j):
+        half = zh_at[j]
+        for o in (1, 3, 2):
+            y_from = rem(y + o, 4)
+            remote(
+                ds.at[0, 0], dyr.at[half, y_from], dy_send, dy_recv + half * 4 + y_from,
+                around_y[o - 1],
+            ).wait_recv()
+        for zl_ in range(4):
+            rows = slice(zl_ * 128, (zl_ + 1) * 128)
+            acc = dyr[half, 0, rows].astype(F32)
+            for y_ in range(1, 4):
+                acc += dyr[half, y_, rows].astype(F32)
+            for x_ in range(4):
+                dxs[j, x_, zl_] = acc[x_ * 32 : (x_ + 1) * 32].astype(BF16)
+        for o in (2, 1, 3):
+            sem = dx_sems + (j * 3 + o - 1) * 2
+            copy = remote(
+                dxs.at[j, rem(x + o, 4)], dxr.at[j, o - 1], sem, sem + 1, around_x[o - 1]
+            )
+            copy.start()
+            pending.append(copy)
+
+    def over_x(j):
+        for o in (1, 3, 2):
+            sem = dx_sems + (j * 3 + o - 1) * 2
+            remote(
+                dxs.at[j, x], dxr.at[j, o - 1], sem, sem + 1, around_x[3 - o]
+            ).wait_recv()
+        acc = dxs[j, x].astype(F32)
+        for o in range(3):
+            acc += dxr[j, o].astype(F32)
+        dzs[j] = acc.astype(BF16)
+        for o in (2, 1, 3, 0):
+            zl_to, half = rem(zl + o, 4), zh_at[j]
+            mine = half == zh
+            copy = remote(
+                dzs.at[j, zl_to], dzr.at[z], dz_send + j * 4 + o, dz_recv + z,
+                at(zl_=zl_to, zh_=half),
+            )
+            if o == 0:
+                pl.when(jnp.logical_not(mine))(copy.start)
+                pending.append((jnp.logical_not(mine), copy))
+
+                @pl.when(mine)
+                def _():
+                    dzr[z] = dzs[j, zl]
+
+            else:
+                copy.start()
+                pending.append(copy)
+
+    arrive_z(1)
     neighbours(0)
-    neighbours(1)
     loads[4].wait()
     a_theirs.wait_recv()
-    partial(0)
-    send_y(0)
+    partial(0, 0)
+    arrive_z(2)
+    share_rows()
+    neighbours(1)
+    partial(1, 0)
+    far(0)
+    partial(0, 1)
+    arrive_z(3)
     neighbours(2)
+    reduce_y(0, 0)
+    partial(2, 0)
+    far(1)
+    partial(1, 1)
+    reduce_y(1, 0)
+    z0 = exchange(0)
     fr_mine.wait()
     for copy in fr_arrive:
         copy.wait_recv()
@@ -364,81 +446,47 @@
     fr_swap = remote(fr.at[:, :, k], fr.at[:, :, k], fr_sems, fr_sems + 1, partner)
     fr_swap.start()
     pending.append(fr_swap)
-    z0 = reduce_y(0)
+    reduce_y(0, 1)
     neighbours(3)
-    partial(1)
-    send_y(1)
-    far(0)
-    far(1)
-    partial(2)
-    send_y(2)
-    z1 = reduce_y(1)
+    partial(3, 0)
+    remote(fr.at[:, :, 1 - k], fr.at[:, :, 1 - k], fr_sems, fr_sems + 1, partner).wait_recv()
+    products(0)
+    far(2)
+    partial(2, 1)
+    reduce_y(1, 1)
+    z2 = exchange(2)
+    products(1)
+    reduce_y(2, 0)
+    far(3)
+    partial(3, 1)
+    reduce_y(3, 0)
+    z1 = exchange(1)
     c0 = finish(0, z0)
-    remote(fr.at[:, :, 1 - k], fr.at[:, :, 1 - k], fr_sems, fr_sems + 1, partner).wait_recv()
+    reduce_y(2, 1)
+    products(2)
+    over_y(0)
+    reduce_y(3, 1)
+    products(3)
+    z3 = exchange(3)
+    over_x(0)
+    c2 = finish(2, z2)
     c1 = finish(1, z1)
-    products(0)
-    z2 = reduce_y(2)
-    far(2)
-    far(3)
-    partial(3)
-    send_y(3)
     write_panel(0, c0)
+    write_panel(2, c2)
+    over_y(1)
+    c3 = finish(3, z3)
     write_panel(1, c1)
-    c2 = finish(2, z2)
-    z3 = reduce_y(3)
-    write_panel(2, c2)
-    c3 = finish(3, z3)
-    products(1)
+    over_x(1)
     write_panel(3, c3)
-
-    def over_y(u):
-        for o in (1, 3, 2):
-            y_from = rem(y + o, 4)
-            remote(
-                ds.at[0, 0], dyr.at[u, y_from], dy_send, dy_recv + u * 4 + y_from,
-                around_y[o - 1],
-            ).wait_recv()
-        for zl_ in range(4):
-            rows = slice(zl_ * 128, (zl_ + 1) * 128)
-            acc = dyr[u, 0, rows].astype(F32)
-            for y_ in range(1, 4):
-                acc += dyr[u, y_, rows].astype(F32)
-            for x_ in range(4):
-                dxs[x_, u, zl_] = acc[x_ * 32 : (x_ + 1) * 32].astype(BF16)
-
-    over_y(u_own)
-    over_y(1 - u_own)
-    arrive = []
-    for o in (1, 3, 2):
-        send, recv = take(), take()
-        copy = remote(dxs.at[rem(x + o, 4)], dxr.at[o - 1], send, recv, around_x[o - 1])
-        copy.start()
-        pending.append(copy)
-        arrive.append(remote(dxs.at[x], dxr.at[o - 1], send, recv, around_x[3 - o]))
-    for copy in arrive:
-        copy.wait_recv()
-    acc = dxs[x].astype(F32)
-    for o in range(3):
-        acc += dxr[o].astype(F32)
-    for zl_ in range(4):
-        dzs[zl_] = acc[:, zl_].astype(BF16)
-    arrive = []
-    for o in (4, 3, 5, 2, 6, 1, 7):
-        z_to, z_from = rem(z + o, 8), rem(z + 8 - o, 8)
-        send, recv = take(), take()
-        copy = remote(dzs.at[rem(z_to, 4)], dzr.at[o - 1], send, recv, chip_z(z_to))
-        copy.start()
-        pending.append(copy)
-        arrive.append(remote(dzs.at[zl], dzr.at[o - 1], send, recv, chip_z(z_from)))
-    for copy in arrive:
-        copy.wait_recv()
-    total = dzs[zl].astype(F32)
-    for o in range(7):
-        total += dzr[o].astype(F32)
-    total = jnp.where(zh == 0, total[:, :, :64], total[:, :, 64:])
+    for o in range(1, 8):
+        z_from = rem(z + o, 8)
+        remote(dzs.at[0, 0], dzr.at[z_from], dz_send, dz_recv + z_from, chip_z(z_from)).wait_recv()
+    total = dzr[0].astype(F32)
+    for z_ in range(1, 8):
+        total += dzr[z_].astype(F32)
     loads[3].wait()
     for s in range(4):
-        diag_ref[s] = inv_ref[s] - total[s // 2, :, (s % 2) * 32 : (s % 2 + 1) * 32]
+        diag_ref[s] = inv_ref[s] + total[:, s * 32 : (s + 1) * 32]
 
     for copy in pending:
         if isinstance(copy, tuple):
@@ -449,7 +497,7 @@
     assert used[0] <= SEMS, used
 
 
-SEMS = 208
+SEMS = 256
 
 
 def per_device(inverse_tiles, factor, inverse_diag, tile_list, tile_count):
@@ -470,23 +518,23 @@
             v((4, 32, 32), F32),
             v((2, 1024, 1024), BF16),
             v((4, 32, 1024), BF16),
-            v((8, 4, 32, 128), BF16),
+            v((4, 4, 32, 256), BF16),
             v((4, 4, 2, 2, 32, 1024), BF16),
-            v((4, 8, 2, 32, 128), BF16),
-            v((4, 2, 4, 128, 256), BF16),
-            v((4, 3, 2, 128, 256), BF16),
+            v((4, 8, 2, 32, 256), BF16),
+            v((8, 2, 4, 128, 128), BF16),
+            v((8, 3, 2, 128, 128), BF16),
+            v((4, 2, 2, 256, 128), BF16),
             v((4, 128, 256), F32),
             v((4, 128, 256), BF16),
             v((4, 128, 256), BF16),
             v((4, 128, 256), BF16),
             v((4, 64, 256), BF16),
+            v((4, 2, 512, 128), BF16),
             v((2, 4, 512, 128), BF16),
-            v((2, 4, 512, 128), BF16),
-            v((4, 2, 4, 32, 128), BF16),
-            v((3, 2, 4, 32, 128), BF16),
-            v((4, 2, 32, 128), BF16),
-            v((7, 2, 32, 128), BF16),
-            v((2, 256, 512), BF16),
+            v((2, 4, 4, 32, 128), BF16),
+            v((2, 3, 4, 32, 128), BF16),
+            v((2, 4, 32, 128), BF16),
+            v((8, 32, 128), BF16),
             v((2, 256, 512), BF16),
             pltpu.SemaphoreType.DMA((SEMS,)),
         ],

time: 110 us -> 104 us (0.945); the launches traced: 110 us -> 103 us
  Pallas kernels: 106 us -> 98.6 us
    pallas_call x1, Pallas kernels: 106 us -> 98.6 us  [per_device(): pl.pallas_call(kernel, out_shape=(jax.ShapeDtypeStruct((64, 2048), BF16),...]
where the time goes in v4:
time: 104 us; the launch traced here: 103 us
  Pallas kernels  98.6 us (95%)
  local copies, waits for them, and re-layouts  3.31 us (3%)
    pallas_call x1, Pallas kernels, per_device(): pl.pallas_call(kernel, out_shape=(jax.ShapeDtypeStruct((64, 2048), BF16),...  98.6 us

profile of v4, /device:TPU:32, one launch (start us, length us, event | category | flops | bytes accessed | tf_op | source)
XLA Modules:
  0.0 102.5 jit_solution(7360162937688331025)
XLA Ops:
  0.6 98.6 %shard_map.68 = (bf16[64,2048]{1,0:T(8,128)(2,1)}, f32[4,32,32]{2,1,0:T(8,128)}) custom-call(s32[4,128]{1,0:T(4,128)} %list_hbm.1, s32[4]{0:T(128)} %count_hbm.1, bf16[1024,1024]{1,0:T(8,128)(2,1)} %a_ref.1, bf16[4,32,1024]{2,1,0:T(8,128)(2,1)} %bitcast.1, f32[4,32,32]{2,1,0:T(8,128)} %inv_hbm.1), custom_call_target="tpu_custom_call" | custom-call | flops 4294967296 | bytes 4194304 | tf_op jit(solution)/shard_map/pallas_call | solution.py:506
  99.2 1.8 %reshape.7 = bf16[64,4,512]{2,1,0:T(4,128)(2,1)} reshape(bf16[64,2048]{1,0:T(8,128)(2,1)} %get-tuple-element.4) | data formatting | bytes 524288 | tf_op jit(solution)/shard_map/reshape | solution.py:548
  101.0 1.5 %copy.8 = f32[4,32,32]{2,1,0:T(8,128)} copy(f32[4,32,32]{2,1,0:T(8,128)} %get-tuple-element.9) | data formatting | bytes 32768

commit v5 on v4

--- a/solution.py
+++ b/solution.py
@@ -58,13 +58,17 @@
 
     u_own = div(x, 2)
     to_zh, to_y = div(zl, 2), rem(zl, 2) * 2 + div(x, 2)
-    to_place, to_yh = zh * 2 + rem(y, 2), div(y, 2)
+    to_place = jnp.where(zh == to_zh, 1 + rem(y, 2), 3 * rem(y, 2))
+    to_yh = div(y, 2)
     here = (to_zh == zh) & (to_y == y) & (to_place == zl)
+
+    def half_of(place):
+        return jnp.where((place == 1) | (place == 2), zh, 1 - zh)
 
     def source(yh):
         return at(
-            x_=jnp.where(u_own == rem(y, 2), x, rem(x + 2, 4)), y_=yh * 2 + rem(zl, 2),
-            zh_=div(zl, 2), zl_=zh * 2 + div(y, 2),
+            x_=jnp.where(u_own == rem(y, 2), x, rem(x + 2, 4)), y_=yh * 2 + div(zl, 2),
+            zh_=half_of(zl), zl_=zh * 2 + div(y, 2),
         )
 
     first = take(5)
@@ -168,13 +172,16 @@
         perm[core] = jnp.where(hit, 1.0, 0.0).astype(BF16)
     line_send, line_recv, pass_send = take(2), take(4), take(3)
     right_send, right_recv, left_send, left_recv = take(4), take(4), take(4), take(4)
-    zh_at = [div(zl, 2), 1 - div(zl, 2)]
+    zh_at = [zh, 1 - zh]
     inner = (zl == 1) | (zl == 2)
     even = rem(zl, 2) == 0
     flip1 = jnp.where(even, zl + 1, zl - 1)
     flip2 = rem(zl + 2, 4)
     flip3 = 3 - zl
-    order = [zl, flip1, jnp.where(inner, flip3, flip2), jnp.where(inner, flip2, flip3)]
+    order = [
+        zl, jnp.where(inner, flip3, flip1), jnp.where(inner, flip1, flip2),
+        jnp.where(inner, flip2, flip3),
+    ]
 
     def along_line(place, sem, to):
         on = (to >= 0) & (to <= 3)
@@ -247,7 +254,8 @@
         remote(part, part, far_left_send, far_left_recv + place, right).wait_recv()
 
     u_of = [u_own, 1 - u_own]
-    b_of = [rem(place, 2) for place in order]
+    b_of = [div(place, 2) for place in order]
+    half_at = [half_of(place) for place in order]
 
     def partial(i, w):
         u, place, c = u_of[w], order[i], i * 2 + w
@@ -294,7 +302,8 @@
             lane_live.append(mask)
 
     def reduce_y(i, w):
-        c, step = i * 2 + w, w * 2 + i // 2
+        c = i * 2 + w
+        step = w * 2 + jnp.where(half_at[i] == zh, 0, 1)
         for o in (1, 3, 2):
             sem = y_sems + (c * 3 + o - 1) * 2
             came = around_y[3 - o]
@@ -315,12 +324,16 @@
         zs[step, :, lanes] = jnp.where(zh == 0, sums[1], sums[0]).astype(BF16)
 
     def exchange(step):
+        other = step + 1 - 2 * (step % 2)
+        device = at(zh_=1 - zh)
         copy = remote(
-            zs.at[step], zr.at[step], z_sems + step * 2, z_sems + step * 2 + 1, at(zh_=1 - zh)
+            zs.at[step], zr.at[other], z_sems + step * 2, z_sems + other * 2 + 1, device
         )
         copy.start()
         pending.append(copy)
-        return copy
+        return remote(
+            zs.at[other], zr.at[step], z_sems + other * 2, z_sems + step * 2 + 1, device
+        )
 
     def finish(step, z_copy):
         z_copy.wait_recv()
@@ -354,7 +367,7 @@
         turned = [pltpu.roll(acc, 64, 1) for acc in both]
         ds[i, 0] = jnp.where(low, both[0], turned[1]).astype(BF16)
         ds[i, 1] = jnp.where(low, turned[0], both[1]).astype(BF16)
-        half = zh_at[i // 2]
+        half = half_at[i]
         for yh in range(2):
             y_to = yh * 2 + b_of[i]
             send = remote(
@@ -403,22 +416,15 @@
         dzs[j] = acc.astype(BF16)
         for o in (2, 1, 3, 0):
             zl_to, half = rem(zl + o, 4), zh_at[j]
-            mine = half == zh
+            if half is zh and o == 0:
+                dzr[z] = dzs[j, zl]
+                continue
             copy = remote(
                 dzs.at[j, zl_to], dzr.at[z], dz_send + j * 4 + o, dz_recv + z,
                 at(zl_=zl_to, zh_=half),
             )
-            if o == 0:
-                pl.when(jnp.logical_not(mine))(copy.start)
-                pending.append((jnp.logical_not(mine), copy))
-
-                @pl.when(mine)
-                def _():
-                    dzr[z] = dzs[j, zl]
-
-            else:
-                copy.start()
-                pending.append(copy)
+            copy.start()
+            pending.append(copy)
 
     arrive_z(1)
     neighbours(0)
@@ -426,18 +432,22 @@
     a_theirs.wait_recv()
     partial(0, 0)
     arrive_z(2)
-    share_rows()
     neighbours(1)
     partial(1, 0)
     far(0)
     partial(0, 1)
     arrive_z(3)
     neighbours(2)
+    share_rows()
     reduce_y(0, 0)
     partial(2, 0)
     far(1)
     partial(1, 1)
     reduce_y(1, 0)
+    reduce_y(0, 1)
+    neighbours(3)
+    partial(3, 0)
+    reduce_y(2, 0)
     z0 = exchange(0)
     fr_mine.wait()
     for copy in fr_arrive:
@@ -446,29 +456,25 @@
     fr_swap = remote(fr.at[:, :, k], fr.at[:, :, k], fr_sems, fr_sems + 1, partner)
     fr_swap.start()
     pending.append(fr_swap)
-    reduce_y(0, 1)
-    neighbours(3)
-    partial(3, 0)
+    reduce_y(1, 1)
+    far(2)
+    partial(2, 1)
     remote(fr.at[:, :, 1 - k], fr.at[:, :, 1 - k], fr_sems, fr_sems + 1, partner).wait_recv()
     products(0)
-    far(2)
-    partial(2, 1)
-    reduce_y(1, 1)
-    z2 = exchange(2)
     products(1)
-    reduce_y(2, 0)
     far(3)
     partial(3, 1)
-    reduce_y(3, 0)
-    z1 = exchange(1)
-    c0 = finish(0, z0)
     reduce_y(2, 1)
     products(2)
     over_y(0)
+    reduce_y(3, 0)
     reduce_y(3, 1)
     products(3)
+    z2 = exchange(2)
+    z1 = exchange(1)
     z3 = exchange(3)
     over_x(0)
+    c0 = finish(0, z0)
     c2 = finish(2, z2)
     c1 = finish(1, z1)
     write_panel(0, c0)

time: 104 us -> 110 us (1.058)
  Pallas kernels: 98.6 us -> 104 us
    pallas_call x1, Pallas kernels: 98.6 us -> 104 us  [per_device(): pl.pallas_call(kernel, out_shape=(jax.ShapeDtypeStruct((64, 2048), BF16),...]
where the time goes in v5:
time: 110 us; the launch traced here: 108 us
  Pallas kernels  104 us (95%)
  local copies, waits for them, and re-layouts  3.31 us (3%)
    pallas_call x1, Pallas kernels, per_device(): pl.pallas_call(kernel, out_shape=(jax.ShapeDtypeStruct((64, 2048), BF16),...  104 us

profile of v5, /device:TPU:32, one launch (start us, length us, event | category | flops | bytes accessed | tf_op | source)
XLA Modules:
  0.0 107.9 jit_solution(9669096502289449046)
XLA Ops:
  0.6 104.0 %shard_map.68 = (bf16[64,2048]{1,0:T(8,128)(2,1)}, f32[4,32,32]{2,1,0:T(8,128)}) custom-call(s32[4,128]{1,0:T(4,128)} %list_hbm.1, s32[4]{0:T(128)} %count_hbm.1, bf16[1024,1024]{1,0:T(8,128)(2,1)} %a_ref.1, bf16[4,32,1024]{2,1,0:T(8,128)(2,1)} %bitcast.1, f32[4,32,32]{2,1,0:T(8,128)} %inv_hbm.1), custom_call_target="tpu_custom_call" | custom-call | flops 4294967296 | bytes 4194304 | tf_op jit(solution)/shard_map/pallas_call | solution.py:512
  104.6 1.8 %reshape.7 = bf16[64,4,512]{2,1,0:T(4,128)(2,1)} reshape(bf16[64,2048]{1,0:T(8,128)(2,1)} %get-tuple-element.4) | data formatting | bytes 524288 | tf_op jit(solution)/shard_map/reshape | solution.py:554
  106.4 1.5 %copy.8 = f32[4,32,32]{2,1,0:T(8,128)} copy(f32[4,32,32]{2,1,0:T(8,128)} %get-tuple-element.9) | data formatting | bytes 32768

commit v6 on v5

--- a/solution.py
+++ b/solution.py
@@ -22,7 +22,7 @@
 def kernel(
     list_hbm, count_hbm, a_ref, ft_hbm, inv_hbm, panel_ref, diag_ref,
     list_ref, count_ref, ft_ref, inv_ref,
-    abuf, fmask, ftile, fg, fr, pp, pyr, sb, zown, zs, zr, pb, cr, ds, dyr, dxs, dxr, dzs,
+    abuf, fmask, ftile, fg, fr, pp, pyr, sb, zown, zs, zr, pb, cr, dxs, dxr, dys, dyr, dzs,
     dzr, perm, sems,
 ):
     row, col = lax.axis_index("row"), lax.axis_index("col")
@@ -287,7 +287,7 @@
     y_sems = take(48)
     z_sems, c_sems = take(8), take(8)
     dy_send, dy_recv = take(8), take(8)
-    dx_sems = take(12)
+    dx_sems = take(24)
     dz_send, dz_recv = take(8), take(8)
 
     lane = lax.broadcasted_iota(jnp.int32, (1, 128), 1)
@@ -365,13 +365,35 @@
                 )
             both.append(acc)
         turned = [pltpu.roll(acc, 64, 1) for acc in both]
-        ds[i, 0] = jnp.where(low, both[0], turned[1]).astype(BF16)
-        ds[i, 1] = jnp.where(low, turned[0], both[1]).astype(BF16)
+        tiles = (jnp.where(low, both[0], turned[1]), jnp.where(low, turned[0], both[1]))
+        for yh in range(2):
+            for zl_ in range(4):
+                for x_ in range(4):
+                    first = zl_ * 128 + x_ * 32
+                    dxs[i, x_, yh, zl_] = tiles[yh][first : first + 32].astype(BF16)
+        for o in (2, 1, 3):
+            sem = dx_sems + (i * 3 + o - 1) * 2
+            copy = remote(
+                dxs.at[i, rem(x + o, 4)], dxr.at[i, o - 1], sem, sem + 1, around_x[o - 1]
+            )
+            copy.start()
+            pending.append(copy)
+
+    def over_x(i):
+        for o in (1, 3, 2):
+            sem = dx_sems + (i * 3 + o - 1) * 2
+            remote(
+                dxs.at[i, x], dxr.at[i, o - 1], sem, sem + 1, around_x[3 - o]
+            ).wait_recv()
+        acc = dxs[i, x].astype(F32)
+        for o in range(3):
+            acc += dxr[i, o].astype(F32)
+        dys[i] = acc.astype(BF16)
         half = half_at[i]
         for yh in range(2):
             y_to = yh * 2 + b_of[i]
             send = remote(
-                ds.at[i, yh], dyr.at[half, y], dy_send + i * 2 + yh, dy_recv + half * 4 + y,
+                dys.at[i, yh], dyr.at[half, y], dy_send + i * 2 + yh, dy_recv + half * 4 + y,
                 at(y_=y_to),
             )
             pl.when(y_to != y)(send.start)
@@ -379,44 +401,23 @@
 
             @pl.when(y_to == y)
             def _():
-                dyr[half, y] = ds[i, yh]
+                dyr[half, y] = dys[i, yh]
 
     def over_y(j):
         half = zh_at[j]
         for o in (1, 3, 2):
             y_from = rem(y + o, 4)
             remote(
-                ds.at[0, 0], dyr.at[half, y_from], dy_send, dy_recv + half * 4 + y_from,
+                dys.at[0, 0], dyr.at[half, y_from], dy_send, dy_recv + half * 4 + y_from,
                 around_y[o - 1],
             ).wait_recv()
-        for zl_ in range(4):
-            rows = slice(zl_ * 128, (zl_ + 1) * 128)
-            acc = dyr[half, 0, rows].astype(F32)
-            for y_ in range(1, 4):
-                acc += dyr[half, y_, rows].astype(F32)
-            for x_ in range(4):
-                dxs[j, x_, zl_] = acc[x_ * 32 : (x_ + 1) * 32].astype(BF16)
-        for o in (2, 1, 3):
-            sem = dx_sems + (j * 3 + o - 1) * 2
-            copy = remote(
-                dxs.at[j, rem(x + o, 4)], dxr.at[j, o - 1], sem, sem + 1, around_x[o - 1]
-            )
-            copy.start()
-            pending.append(copy)
-
-    def over_x(j):
-        for o in (1, 3, 2):
-            sem = dx_sems + (j * 3 + o - 1) * 2
-            remote(
-                dxs.at[j, x], dxr.at[j, o - 1], sem, sem + 1, around_x[3 - o]
-            ).wait_recv()
-        acc = dxs[j, x].astype(F32)
-        for o in range(3):
-            acc += dxr[j, o].astype(F32)
+        acc = dyr[half, 0].astype(F32)
+        for y_ in range(1, 4):
+            acc += dyr[half, y_].astype(F32)
         dzs[j] = acc.astype(BF16)
         for o in (2, 1, 3, 0):
-            zl_to, half = rem(zl + o, 4), zh_at[j]
-            if half is zh and o == 0:
+            zl_to = rem(zl + o, 4)
+            if j == 0 and o == 0:
                 dzr[z] = dzs[j, zl]
                 continue
             copy = remote(
@@ -437,8 +438,8 @@
     far(0)
     partial(0, 1)
     arrive_z(3)
+    share_rows()
     neighbours(2)
-    share_rows()
     reduce_y(0, 0)
     partial(2, 0)
     far(1)
@@ -448,6 +449,9 @@
     neighbours(3)
     partial(3, 0)
     reduce_y(2, 0)
+    reduce_y(1, 1)
+    far(2)
+    partial(2, 1)
     z0 = exchange(0)
     fr_mine.wait()
     for copy in fr_arrive:
@@ -456,33 +460,32 @@
     fr_swap = remote(fr.at[:, :, k], fr.at[:, :, k], fr_sems, fr_sems + 1, partner)
     fr_swap.start()
     pending.append(fr_swap)
-    reduce_y(1, 1)
-    far(2)
-    partial(2, 1)
+    far(3)
+    partial(3, 1)
+    reduce_y(3, 0)
+    z1 = exchange(1)
+    reduce_y(2, 1)
+    z2 = exchange(2)
     remote(fr.at[:, :, 1 - k], fr.at[:, :, 1 - k], fr_sems, fr_sems + 1, partner).wait_recv()
     products(0)
     products(1)
-    far(3)
-    partial(3, 1)
-    reduce_y(2, 1)
+    reduce_y(3, 1)
     products(2)
-    over_y(0)
-    reduce_y(3, 0)
-    reduce_y(3, 1)
     products(3)
-    z2 = exchange(2)
-    z1 = exchange(1)
     z3 = exchange(3)
     over_x(0)
+    over_x(1)
     c0 = finish(0, z0)
+    over_x(2)
     c2 = finish(2, z2)
+    over_y(0)
     c1 = finish(1, z1)
+    over_x(3)
     write_panel(0, c0)
     write_panel(2, c2)
     over_y(1)
     c3 = finish(3, z3)
     write_panel(1, c1)
-    over_x(1)
     write_panel(3, c3)
     for o in range(1, 8):
         z_from = rem(z + o, 8)
@@ -503,7 +506,7 @@
     assert used[0] <= SEMS, used
 
 
-SEMS = 256
+SEMS = 264
 
 
 def per_device(inverse_tiles, factor, inverse_diag, tile_list, tile_count):
@@ -535,10 +538,10 @@
             v((4, 128, 256), BF16),
             v((4, 128, 256), BF16),
             v((4, 64, 256), BF16),
-            v((4, 2, 512, 128), BF16),
-            v((2, 4, 512, 128), BF16),
+            v((4, 4, 2, 4, 32, 128), BF16),
+            v((4, 3, 2, 4, 32, 128), BF16),
+            v((4, 2, 4, 32, 128), BF16),
             v((2, 4, 4, 32, 128), BF16),
-            v((2, 3, 4, 32, 128), BF16),
             v((2, 4, 32, 128), BF16),
             v((8, 32, 128), BF16),
             v((2, 256, 512), BF16),

time: 110 us -> 100 us (0.909); the launches traced: 108 us -> 100 us
  Pallas kernels: 104 us -> 96.1 us
    pallas_call x1, Pallas kernels: 104 us -> 96.1 us  [per_device(): pl.pallas_call(kernel, out_shape=(jax.ShapeDtypeStruct((64, 2048), BF16),...]
where the time goes in v6:
time: 100 us
  Pallas kernels  96.1 us (96%)
  local copies, waits for them, and re-layouts  3.31 us (3%)
    pallas_call x1, Pallas kernels, per_device(): pl.pallas_call(kernel, out_shape=(jax.ShapeDtypeStruct((64, 2048), BF16),...  96.1 us

profile of v6, /device:TPU:32, one launch (start us, length us, event | category | flops | bytes accessed | tf_op | source)
XLA Modules:
  0.0 100.0 jit_solution(15712912417980972537)
XLA Ops:
  0.6 96.1 %shard_map.68 = (bf16[64,2048]{1,0:T(8,128)(2,1)}, f32[4,32,32]{2,1,0:T(8,128)}) custom-call(s32[4,128]{1,0:T(4,128)} %list_hbm.1, s32[4]{0:T(128)} %count_hbm.1, bf16[1024,1024]{1,0:T(8,128)(2,1)} %a_ref.1, bf16[4,32,1024]{2,1,0:T(8,128)(2,1)} %bitcast.1, f32[4,32,32]{2,1,0:T(8,128)} %inv_hbm.1), custom_call_target="tpu_custom_call" | custom-call | flops 4294967296 | bytes 4194304 | tf_op jit(solution)/shard_map/pallas_call | solution.py:515
  96.7 1.8 %reshape.7 = bf16[64,4,512]{2,1,0:T(4,128)(2,1)} reshape(bf16[64,2048]{1,0:T(8,128)(2,1)} %get-tuple-element.4) | data formatting | bytes 524288 | tf_op jit(solution)/shard_map/reshape | solution.py:557
  98.5 1.5 %copy.8 = f32[4,32,32]{2,1,0:T(8,128)} copy(f32[4,32,32]{2,1,0:T(8,128)} %get-tuple-element.9) | data formatting | bytes 32768

commit v7 on v6

--- a/solution.py
+++ b/solution.py
@@ -71,12 +71,15 @@
             zh_=half_of(zl), zl_=zh * 2 + div(y, 2),
         )
 
+    def lanes_of(core):
+        return pl.ds(pl.multiple_of(core * 1024, 1024), 1024)
+
     first = take(5)
     loads = [
         pltpu.make_async_copy(src, dst, sems.at[first + i])
         for i, (src, dst) in enumerate(
             ((ft_hbm, ft_ref), (list_hbm, list_ref), (count_hbm, count_ref), (inv_hbm, inv_ref),
-             (a_ref, abuf.at[k]))
+             (a_ref, abuf.at[:, lanes_of(k)]))
         )
     ]
     for copy in loads:
@@ -157,10 +160,10 @@
     pending.append((jnp.logical_not(here), remote_kept))
 
     a_sems = take(2)
-    a_swap = remote(a_ref, abuf.at[k], a_sems, a_sems + 1, partner)
+    a_swap = remote(a_ref, abuf.at[:, lanes_of(k)], a_sems, a_sems + 1, partner)
     a_swap.start()
     pending.append(a_swap)
-    a_theirs = remote(a_ref, abuf.at[1 - k], a_sems, a_sems + 1, partner)
+    a_theirs = remote(a_ref, abuf.at[:, lanes_of(1 - k)], a_sems, a_sems + 1, partner)
 
     r_iota = lax.broadcasted_iota(jnp.int32, (256, 512), 0)
     c_iota = lax.broadcasted_iota(jnp.int32, (256, 512), 1)
@@ -260,22 +263,12 @@
     def partial(i, w):
         u, place, c = u_of[w], order[i], i * 2 + w
 
-        def body(n, carry):
-            rows = pl.ds(pl.multiple_of(n * 256, 256), 256)
-            acc = lax.dot_general(
-                abuf[0, rows], fg[2 * u, place].reshape(128, 1024), NT_DIMS,
-                preferred_element_type=F32,
-            )
-            acc += lax.dot_general(
-                abuf[1, rows], fg[2 * u + 1, place].reshape(128, 1024), NT_DIMS,
-                preferred_element_type=F32,
-            )
-            first = rem(n, 2) * 2
-            for j in range(2):
-                pp[c, div(n, 2), first + j] = acc[j * 128 : (j + 1) * 128].astype(BF16)
-            return carry
-
-        lax.fori_loop(0, 4, body, 0)
+        block = jnp.concatenate(
+            [fg[2 * u + h, place].reshape(128, 1024) for h in range(2)], axis=1
+        )
+        acc = lax.dot_general(abuf[...], block, NT_DIMS, preferred_element_type=F32)
+        for j in range(8):
+            pp[c, j // 4, j % 4] = acc[j * 128 : (j + 1) * 128].astype(BF16)
         for o in (2, 1, 3):
             sem = y_sems + (c * 3 + o - 1) * 2
             copy = remote(
@@ -525,7 +518,7 @@
             pltpu.SMEM((4,), jnp.int32),
             v((4, 32, 1024), BF16),
             v((4, 32, 32), F32),
-            v((2, 1024, 1024), BF16),
+            v((1024, 2048), BF16),
             v((4, 32, 1024), BF16),
             v((4, 4, 32, 256), BF16),
             v((4, 4, 2, 2, 32, 1024), BF16),

time: 100 us -> 98.2 us (0.982)
  Pallas kernels: 96.1 us -> 93.3 us
    pallas_call x1, Pallas kernels: 96.1 us -> 93.3 us  [per_device(): pl.pallas_call(kernel, out_shape=(jax.ShapeDtypeStruct((64, 2048), BF16),...]
where the time goes in v7:
time: 98.2 us; the launch traced here: 97.2 us
  Pallas kernels  93.3 us (95%)
  local copies, waits for them, and re-layouts  3.31 us (3%)
    pallas_call x1, Pallas kernels, per_device(): pl.pallas_call(kernel, out_shape=(jax.ShapeDtypeStruct((64, 2048), BF16),...  93.3 us

profile of v7, /device:TPU:32, one launch (start us, length us, event | category | flops | bytes accessed | tf_op | source)
XLA Modules:
  0.0 97.2 jit_solution(17105956434390612352)
XLA Ops:
  0.6 93.3 %shard_map.68 = (bf16[64,2048]{1,0:T(8,128)(2,1)}, f32[4,32,32]{2,1,0:T(8,128)}) custom-call(s32[4,128]{1,0:T(4,128)} %list_hbm.1, s32[4]{0:T(128)} %count_hbm.1, bf16[1024,1024]{1,0:T(8,128)(2,1)} %a_ref.1, bf16[4,32,1024]{2,1,0:T(8,128)(2,1)} %bitcast.1, f32[4,32,32]{2,1,0:T(8,128)} %inv_hbm.1), custom_call_target="tpu_custom_call" | custom-call | flops 4294967296 | bytes 4194304 | tf_op jit(solution)/shard_map/pallas_call | solution.py:508
  93.9 1.8 %reshape.7 = bf16[64,4,512]{2,1,0:T(4,128)(2,1)} reshape(bf16[64,2048]{1,0:T(8,128)(2,1)} %get-tuple-element.4) | data formatting | bytes 524288 | tf_op jit(solution)/shard_map/reshape | solution.py:550
  95.8 1.5 %copy.8 = f32[4,32,32]{2,1,0:T(8,128)} copy(f32[4,32,32]{2,1,0:T(8,128)} %get-tuple-element.9) | data formatting | bytes 32768

commit v8 on v7

--- a/solution.py
+++ b/solution.py
@@ -428,9 +428,9 @@
     arrive_z(2)
     neighbours(1)
     partial(1, 0)
+    arrive_z(3)
     far(0)
     partial(0, 1)
-    arrive_z(3)
     share_rows()
     neighbours(2)
     reduce_y(0, 0)

time: 98.2 us -> 101 us (1.029); the launches traced: 97.2 us -> 101 us
  Pallas kernels: 93.3 us -> 97.3 us
    pallas_call x1, Pallas kernels: 93.3 us -> 97.3 us  [per_device(): pl.pallas_call(kernel, out_shape=(jax.ShapeDtypeStruct((64, 2048), BF16),...]
where the time goes in v8:
time: 101 us
  Pallas kernels  97.3 us (96%)
  local copies, waits for them, and re-layouts  3.31 us (3%)
    pallas_call x1, Pallas kernels, per_device(): pl.pallas_call(kernel, out_shape=(jax.ShapeDtypeStruct((64, 2048), BF16),...  97.3 us

profile of v8, /device:TPU:32, one launch (start us, length us, event | category | flops | bytes accessed | tf_op | source)
XLA Modules:
  0.0 101.3 jit_solution(6510467042951429747)
XLA Ops:
  0.6 97.3 %shard_map.68 = (bf16[64,2048]{1,0:T(8,128)(2,1)}, f32[4,32,32]{2,1,0:T(8,128)}) custom-call(s32[4,128]{1,0:T(4,128)} %list_hbm.1, s32[4]{0:T(128)} %count_hbm.1, bf16[1024,1024]{1,0:T(8,128)(2,1)} %a_ref.1, bf16[4,32,1024]{2,1,0:T(8,128)(2,1)} %bitcast.1, f32[4,32,32]{2,1,0:T(8,128)} %inv_hbm.1), custom_call_target="tpu_custom_call" | custom-call | flops 4294967296 | bytes 4194304 | tf_op jit(solution)/shard_map/pallas_call | solution.py:508
  98.0 1.8 %reshape.7 = bf16[64,4,512]{2,1,0:T(4,128)(2,1)} reshape(bf16[64,2048]{1,0:T(8,128)(2,1)} %get-tuple-element.4) | data formatting | bytes 524288 | tf_op jit(solution)/shard_map/reshape | solution.py:550
  99.8 1.5 %copy.8 = f32[4,32,32]{2,1,0:T(8,128)} copy(f32[4,32,32]{2,1,0:T(8,128)} %get-tuple-element.9) | data formatting | bytes 32768
